TPU v7x, 256 devices: a whole 4x4x8 slice. The times are simulated.
256 devices in a mesh: ctx: 32 (over x, z), head: 8 (over y, core).
Axes of the slice: x: 4, y: 4, z: 8, core: 2. Of those that a mesh axis runs over, the one named last changes fastest.
Arguments:
- query: bfloat16 [32768, 8192], P('ctx', 'head'), may hold values from -6 to 6
- key_in: bfloat16 [32768, 8192], P('ctx', 'head'), may hold values from -6 to 6
- value_in: bfloat16 [32768, 8192], P('ctx', 'head'), may hold values from -6 to 6
- gate_in: bfloat16 [32768, 8192], P('ctx', 'head'), may hold values from -6 to 6
- norm_gain: float32 [8192], P('head'), may hold values from 0.1 to 1.9
- decay_rate: float32 [64], P('head'), may hold values from 0 to 1, as said below
- request_starts: int32 [32], replicated, may hold values from 0 to 32767, as said below
- request_slots: int32 [32], replicated, may hold values from 0 to 31, each once
Outputs:
- normed_output: bfloat16 [32768, 8192], P('ctx', 'head')
- final_states: bfloat16 [32, 64, 128, 128], P('ctx', 'head')
Inputs may be any that keep to these rules, and one draw needn't show every extreme that they name: request_starts rises, its first entry is 0, and the last request runs to the stream's last token. Each aligned block of 1024 tokens holds the last tokens of at most 2 requests, and some block holds exactly 2. `request_slots`: each value once. Request r's decode owner is ctx rank request_slots[r]. `decay_rate`: positive rates.
All inputs are finite; a program needn't handle non-finite values.
Results may differ from a plain program's by a relative error of at most 0.0034.
Values may be sent and summed in bfloat16 or wider, within the bound.
No kernel may reach another device: no remote copies, remote signals or barrier semaphores. Data moves between devices by JAX's collectives and lax.ppermute only.
A program may use at most 128 MiB of HBM per device.

v0:
```python
import functools

import jax
import jax.numpy as jnp
from jax import lax
from jax.experimental import pallas as pl
from jax.experimental.pallas import tpu as pltpu
from jax.sharding import PartitionSpec as P

E = 128
ENDS_MOST = 2
SEGS = ENDS_MOST + 1
BLOCK = 512
TILE = 256
ABSENT = 1 << 20
FAR = 1e38
LOG2E = 1.4426950408889634
norm_eps = 1e-06
MIB = 1 << 20
LIMIT = 62 * MIB
ROOM = 44 * MIB
f32 = jnp.float32
bf16 = jnp.bfloat16
SMEM = pl.BlockSpec(memory_space=pltpu.SMEM)
VMEM = pl.BlockSpec(memory_space=pltpu.VMEM)
HBM = pl.BlockSpec(memory_space=pltpu.HBM)


def silu(values):
    half = values.astype(f32) * 0.5
    return (half + half * jnp.tanh(half)).astype(bf16)


def rate_of(rates_ref, head):
    return jnp.maximum(rates_ref[head], 1e-30)


def end_of(starts_ref, request, stream):
    count = starts_ref.shape[0]
    following = starts_ref[jnp.minimum(request + 1, count - 1)]
    return jnp.where(request < count - 1, following - 1, stream - 1)


def local_ends(starts_ref, rows, ranks):
    stream = rows * ranks
    offset = lax.axis_index("ctx") * rows
    count = starts_ref.shape[0]
    first = jnp.int32(0)
    for request in range(count - 1):
        first += (starts_ref[request + 1] - 1 < offset).astype(jnp.int32)
    end_a = end_of(starts_ref, first, stream) - offset
    end_b = end_of(starts_ref, first + 1, stream) - offset
    end_b = jnp.where(first + 1 < count, end_b, ABSENT)
    return end_a, end_b


def power_of(rates_ref, head):
    return rate_of(rates_ref, head) * -LOG2E


def scalar_exp2(value):
    return jnp.exp2(jnp.full((1, E), value, f32))


def scalar_exp(value):
    return jnp.exp(jnp.full((1, E), value, f32))


def lanes(head):
    return pl.ds(pl.multiple_of(head * E, E), E)


def states_kernel(
    rows, ranks, starts_hbm, rates_hbm, k_hbm, v_hbm, sums_hbm, mid_hbm,
    starts_ref, rates_ref, k_raw, v_raw, gap, masks, sums, mids, sems, arrived, left,
):
    heads = k_raw.shape[1] // E
    small = (
        pltpu.make_async_copy(starts_hbm, starts_ref, sems.at[0]),
        pltpu.make_async_copy(rates_hbm, rates_ref, sems.at[1]),
    )

    def load(head):
        at = lanes(head)
        return (
            pltpu.make_async_copy(k_hbm.at[:, at], k_raw.at[:, at], arrived.at[0, head]),
            pltpu.make_async_copy(v_hbm.at[:, at], v_raw.at[:, at], arrived.at[1, head]),
        )

    share = sums.shape[0] // heads

    def store(head):
        pieces = pl.ds(head * share, share)
        return (
            pltpu.make_async_copy(sums.at[pieces], sums_hbm.at[pieces], left.at[0, head]),
            pltpu.make_async_copy(mids.at[head], mid_hbm.at[head], left.at[1, head]),
        )

    for copy in small:
        copy.start()
    for head in range(heads):
        for copy in load(head):
            copy.start()
    for copy in small:
        copy.wait()
    end_a, end_b = local_ends(starts_ref, rows, ranks)
    token = lax.broadcasted_iota(jnp.int32, (rows, E), 0)
    in_a = token <= end_a
    in_b = token <= end_b
    seg_end = jnp.where(in_a, end_a, jnp.where(in_b, end_b, ABSENT))
    block_end = (token // BLOCK) * BLOCK + (BLOCK - 1)
    gap[...] = (jnp.minimum(seg_end, block_end) - token).astype(f32)
    masks[0] = jnp.where(in_a, 1.0, 0.0).astype(bf16)
    masks[1] = jnp.where(in_b, jnp.where(in_a, 0.0, 1.0), 0.0).astype(bf16)
    masks[2] = jnp.where(in_b, 0.0, 1.0).astype(bf16)
    at_mid = (end_a < BLOCK - 1).astype(jnp.int32) + (end_b < BLOCK - 1).astype(jnp.int32)

    @pl.loop(0, heads)
    def _(head):
        at = lanes(head)
        power = power_of(rates_ref, head)
        for copy in load(head):
            copy.wait()
        parts = []
        for first in range(0, rows, BLOCK):
            span = pl.ds(first, BLOCK)
            keys = silu(k_raw[span, at])
            values = silu(v_raw[span, at])
            scaled = (keys.astype(f32) * jnp.exp2(gap[span, :] * power)).astype(bf16)
            spread = jnp.concatenate([values * masks[x, span, :] for x in range(SEGS)], axis=1)
            parts.append(
                lax.dot_general(
                    scaled, spread, (((0,), (0,)), ((), ())), preferred_element_type=f32
                )
            )
        early, late = parts
        mid = jnp.zeros((E, E), f32)
        for x, end in enumerate((end_a, end_b, jnp.int32(ABSENT))):
            reach = jnp.maximum(jnp.minimum(end, rows - 1) - (BLOCK - 1), 0).astype(f32)
            cols = slice(x * E, (x + 1) * E)
            total = early[:, cols] * scalar_exp2(reach * power) + late[:, cols]
            sums[pl.ds(head * share, share), x] = total.astype(bf16).reshape(share, -1, E)
            mid += early[:, cols] * (at_mid == x).astype(f32)
        mids[head] = mid
        for copy in store(head):
            copy.start()

    for head in range(heads):
        for copy in store(head):
            copy.wait()


def request_ends(starts_ref, rows, ranks):
    count = starts_ref.shape[0]
    ends = [
        starts_ref[r + 1] - 1 if r + 1 < count else jnp.int32(rows * ranks - 1)
        for r in range(count)
    ]
    return ends, [end // rows for end in ends]


def advance(rows, rate, homes, got_ref, counts, keep):
    ranks = got_ref.shape[0]
    for p in range(ranks):
        counts[p] = 0
    for home in homes:
        counts[home] = counts[home] + 1
    whole = scalar_exp(float(rows) * -rate)
    state = jnp.zeros(got_ref.shape[2:], f32)
    for p in range(ranks):
        keep(p, state)
        ended = counts[p]
        state = got_ref[p, ended].astype(f32) + state * (whole * (ended == 0).astype(f32))


def my_rate(rates_ref, ranks):
    return rate_of(rates_ref, lax.axis_index("ctx") * rates_ref.shape[0] // ranks)


def scan_kernel(
    rows, starts_ref, slots_ref, rates_ref, got_ref, back_ref, counts, carried
):
    ranks = got_ref.shape[0]
    rate = my_rate(rates_ref, ranks)
    ends, homes = request_ends(starts_ref, rows, ranks)

    def keep(p, state):
        carried[p] = state
        back_ref[p, 0] = state.astype(bf16)

    advance(rows, rate, homes, got_ref, counts, keep)
    for r, (end, home) in enumerate(zip(ends, homes)):
        second = home == homes[r - 1] if r else jnp.bool_(False)
        lead = scalar_exp((end - home * rows + 1).astype(f32) * -rate)
        lead = lead * jnp.where(second, 0.0, 1.0)
        final = got_ref[home, second.astype(jnp.int32)].astype(f32) + carried[home] * lead
        back_ref[slots_ref[r], 1] = final.astype(bf16)


def inner_kernel(
    rows, ranks, starts_ref, rates_ref, q_hbm, k_hbm, v_hbm, inner_hbm, act_hbm,
    q_raw, k_raw, v_raw, inner, act, dist, arrived, left,
):
    heads = q_raw.shape[1] // E

    def load(head):
        at = lanes(head)
        return (
            pltpu.make_async_copy(q_hbm.at[:, at], q_raw.at[:, at], arrived.at[0, head]),
            pltpu.make_async_copy(k_hbm.at[:, at], k_raw.at[:, at], arrived.at[1, head]),
            pltpu.make_async_copy(v_hbm.at[:, at], v_raw.at[:, at], arrived.at[2, head]),
        )

    def store(head):
        at = lanes(head)
        return (
            pltpu.make_async_copy(inner.at[:, at], inner_hbm.at[:, at], left.at[0, head]),
            pltpu.make_async_copy(act.at[:, at], act_hbm.at[:, at], left.at[1, head]),
        )

    for head in range(heads):
        for copy in load(head):
            copy.start()
    end_a, end_b = local_ends(starts_ref, rows, ranks)
    for block in range(rows // BLOCK):
        t = lax.broadcasted_iota(jnp.int32, (BLOCK, BLOCK), 0)
        s = lax.broadcasted_iota(jnp.int32, (BLOCK, BLOCK), 1)
        here = t + block * BLOCK
        begin = jnp.where(here <= end_a, 0, jnp.where(here <= end_b, end_a + 1, end_b + 1))
        keep = (s <= t) & (s + block * BLOCK >= begin)
        dist[block] = jnp.where(keep, (t - s).astype(f32), FAR)

    @pl.loop(0, heads)
    def _(head):
        at = lanes(head)
        power = power_of(rates_ref, head)
        for copy in load(head):
            copy.wait()
        act[:, at] = silu(q_raw[:, at])
        keys = silu(k_raw[:, at])
        values = silu(v_raw[:, at])
        for block in range(rows // BLOCK):
            base = block * BLOCK
            for top in range(0, BLOCK, TILE):
                wide = top + TILE
                mine = pl.ds(base + top, TILE)
                scores = lax.dot_general(
                    act[mine, at],
                    keys[base : base + wide],
                    (((1,), (1,)), ((), ())),
                    preferred_element_type=f32,
                )
                decay = jnp.exp2(dist[block, top : top + TILE, :wide] * power)
                weights = (scores * decay).astype(bf16)
                inner[mine, at] = jnp.dot(
                    weights, values[base : base + wide], preferred_element_type=f32
                )
        for copy in store(head):
            copy.start()

    for head in range(heads):
        for copy in store(head):
            copy.wait()


def outer_kernel(
    rows, ranks, starts_hbm, rates_hbm, back_hbm, mid_hbm, act_hbm, inner_hbm,
    out_ref, final_hbm, squares_ref,
    starts_ref, rates_ref, back, mid, act, inner, total, arrived, left,
):
    heads = mid.shape[0]
    share = back.shape[0] // heads

    def load(head):
        at = lanes(head)
        return (
            pltpu.make_async_copy(act_hbm.at[:, at], act.at[:, at], arrived.at[0, head]),
            pltpu.make_async_copy(inner_hbm.at[:, at], inner.at[:, at], arrived.at[1, head]),
        )

    whole = (
        pltpu.make_async_copy(starts_hbm, starts_ref, arrived.at[0, heads + 1]),
        pltpu.make_async_copy(rates_hbm, rates_ref, arrived.at[1, heads + 1]),
        pltpu.make_async_copy(back_hbm, back, arrived.at[0, heads]),
        pltpu.make_async_copy(mid_hbm, mid, arrived.at[1, heads]),
    )
    finals = pltpu.make_async_copy(back.at[:, 1], final_hbm, left.at[0])
    for copy in whole:
        copy.start()
    for head in range(heads):
        for copy in load(head):
            copy.start()
    for copy in whole:
        copy.wait()
    finals.start()
    end_a, end_b = local_ends(starts_ref, rows, ranks)
    mid_end = jnp.where(end_a >= BLOCK - 1, end_a, jnp.where(end_b >= BLOCK - 1, end_b, ABSENT))
    from_before = (end_a >= BLOCK - 1).astype(f32)
    total[...] = jnp.zeros_like(total)

    @pl.loop(0, heads)
    def _(head):
        at = lanes(head)
        power = power_of(rates_ref, head)
        incoming = back[pl.ds(head * share, share), 0].reshape(E, E)
        later = mid[head] + incoming.astype(f32) * (scalar_exp2(float(BLOCK) * power) * from_before)
        steps = lax.broadcasted_iota(jnp.int32, (BLOCK, E), 0)
        reach = jnp.exp2((steps + 1).astype(f32) * power)
        for copy in load(head):
            copy.wait()
        for block, (state, last) in enumerate(((incoming, end_a), (later.astype(bf16), mid_end))):
            span = pl.ds(block * BLOCK, BLOCK)
            outer = jnp.dot(act[span, at], state, preferred_element_type=f32)
            lead = jnp.where(steps + block * BLOCK <= last, reach, 0.0)
            attended = inner[span, at] + outer * lead
            out_ref[span, at] = attended
            total[span, :] += attended * attended

    row_sums = jnp.concatenate(
        [
            jnp.sum(total[first : first + E, :].T, axis=0, keepdims=True)
            for first in range(0, rows, E)
        ],
        axis=0,
    )
    squares_ref[...] = jnp.broadcast_to(row_sums[None], squares_ref.shape)
    finals.wait()


def norm_kernel(
    features, squares_ref, gain_ref, att_ref, gate_hbm, out_hbm, gate, out, sems
):
    bands = out.shape[0] // E

    def load(band):
        span = pl.ds(band * E, E)
        return pltpu.make_async_copy(gate_hbm.at[span, :], gate.at[span, :], sems.at[0, band])

    def store(band):
        span = pl.ds(band * E, E)
        return pltpu.make_async_copy(out.at[span, :], out_hbm.at[span, :], sems.at[1, band])

    for band in range(bands):
        load(band).start()
    total = jnp.sum(squares_ref[...], axis=0)
    scale = lax.rsqrt(total * (1.0 / features) + norm_eps)
    for band in range(bands):
        span = pl.ds(band * E, E)
        column = jnp.broadcast_to(scale[band : band + 1], (E, E)).T
        load(band).wait()
        for first in range(0, out.shape[1], E):
            cols = slice(first, first + E)
            opened = 0.5 + 0.5 * jnp.tanh(0.5 * gate[span, cols].astype(f32))
            scaled = att_ref[span, cols] * column * gain_ref[:, cols]
            out[span, cols] = (scaled * opened).astype(bf16)
        store(band).start()
    for band in range(bands):
        store(band).wait()


def cost(flops, moved, hard):
    return pl.CostEstimate(flops=int(flops), bytes_accessed=int(moved), transcendentals=int(hard))


def swap(array, axis):
    return lax.all_to_all(array, axis, split_axis=0, concat_axis=0, tiled=True)


def per_device(
    query, key_in, value_in, gate_in, norm_gain, decay_rate, request_starts, request_slots
):
    return local(
        lax.axis_size("ctx"), lax.axis_size("head"), query, key_in, value_in, gate_in, norm_gain,
        decay_rate, request_starts, request_slots,
    )


def local(
    ranks, groups, query, key_in, value_in, gate_in, norm_gain, decay_rate, request_starts,
    request_slots,
):
    rows, width = query.shape
    heads = decay_rate.shape[0]
    piece = E * heads // ranks

    sums, mid = pl.pallas_call(
        functools.partial(states_kernel, rows, ranks),
        out_shape=(
            jax.ShapeDtypeStruct((ranks, SEGS, piece, E), bf16),
            jax.ShapeDtypeStruct((heads, E, E), f32),
        ),
        in_specs=[HBM, HBM, HBM, HBM],
        out_specs=(HBM, HBM),
        scratch_shapes=[
            pltpu.SMEM(request_starts.shape, jnp.int32),
            pltpu.SMEM(decay_rate.shape, f32),
            pltpu.VMEM((rows, width), bf16),
            pltpu.VMEM((rows, width), bf16),
            pltpu.VMEM((rows, E), f32),
            pltpu.VMEM((SEGS, rows, E), bf16),
            pltpu.VMEM((ranks, SEGS, piece, E), bf16),
            pltpu.VMEM((heads, E, E), f32),
            pltpu.SemaphoreType.DMA((2,)),
            pltpu.SemaphoreType.DMA((2, heads)),
            pltpu.SemaphoreType.DMA((2, heads)),
        ],
        compiler_params=pltpu.CompilerParams(vmem_limit_bytes=LIMIT),
        cost_estimate=cost(2 * rows * width * E * SEGS, 5 * MIB, 3 * rows * width),
        name="states",
    )(request_starts, decay_rate, key_in, value_in)

    got = swap(sums, "ctx")

    inner, act = pl.pallas_call(
        functools.partial(inner_kernel, rows, ranks),
        out_shape=(
            jax.ShapeDtypeStruct((rows, width), f32),
            jax.ShapeDtypeStruct((rows, width), bf16),
        ),
        in_specs=[SMEM, SMEM, HBM, HBM, HBM],
        out_specs=(HBM, HBM),
        scratch_shapes=[
            pltpu.VMEM((rows, width), bf16),
            pltpu.VMEM((rows, width), bf16),
            pltpu.VMEM((rows, width), bf16),
            pltpu.VMEM((rows, width), f32),
            pltpu.VMEM((rows, width), bf16),
            pltpu.VMEM((rows // BLOCK, BLOCK, BLOCK), f32),
            pltpu.SemaphoreType.DMA((3, heads)),
            pltpu.SemaphoreType.DMA((2, heads)),
        ],
        compiler_params=pltpu.CompilerParams(vmem_limit_bytes=LIMIT),
        cost_estimate=cost(4 * rows * width * BLOCK, 12 * rows * width, rows * width * 8),
        name="inner",
    )(request_starts, decay_rate, query, key_in, value_in)

    back = pl.pallas_call(
        functools.partial(scan_kernel, rows),
        out_shape=jax.ShapeDtypeStruct((ranks, 2, piece, E), bf16),
        in_specs=[SMEM, SMEM, SMEM, VMEM],
        out_specs=VMEM,
        scratch_shapes=[pltpu.SMEM((ranks,), jnp.int32), pltpu.VMEM((ranks, piece, E), f32)],
        compiler_params=pltpu.CompilerParams(vmem_limit_bytes=8 * MIB),
        cost_estimate=cost(MIB, 2 * MIB, 0),
        name="scan",
    )(request_starts, request_slots, decay_rate, got)

    returned = swap(back, "ctx")

    attended, final_states, squares = pl.pallas_call(
        functools.partial(outer_kernel, rows, ranks),
        out_shape=(
            jax.ShapeDtypeStruct((rows, width), f32),
            jax.ShapeDtypeStruct((ranks, piece, E), bf16),
            jax.ShapeDtypeStruct((groups, rows // E, E), f32),
        ),
        in_specs=[HBM] * 6,
        out_specs=(VMEM, HBM, VMEM),
        scratch_shapes=[
            pltpu.SMEM(request_starts.shape, jnp.int32),
            pltpu.SMEM(decay_rate.shape, f32),
            pltpu.VMEM((ranks, 2, piece, E), bf16),
            pltpu.VMEM((heads, E, E), f32),
            pltpu.VMEM((rows, width), bf16),
            pltpu.VMEM((rows, width), f32),
            pltpu.VMEM((rows, E), f32),
            pltpu.SemaphoreType.DMA((2, heads + 2)),
            pltpu.SemaphoreType.DMA((1,)),
        ],
        compiler_params=pltpu.CompilerParams(vmem_limit_bytes=ROOM),
        cost_estimate=cost(2 * rows * width * E, 10 * MIB, MIB),
        name="outer",
    )(request_starts, decay_rate, returned, mid, act, inner)

    shared = swap(squares, "head")

    normed_output = pl.pallas_call(
        functools.partial(norm_kernel, float(width * groups)),
        out_shape=jax.ShapeDtypeStruct((rows, width), bf16),
        in_specs=[VMEM, VMEM, VMEM, HBM],
        out_specs=HBM,
        scratch_shapes=[
            pltpu.VMEM((rows, width), bf16),
            pltpu.VMEM((rows, width), bf16),
            pltpu.SemaphoreType.DMA((2, rows // E)),
        ],
        compiler_params=pltpu.CompilerParams(vmem_limit_bytes=ROOM),
        cost_estimate=cost(6 * rows * width, 8 * MIB, rows * width),
        name="norm",
    )(shared, norm_gain.reshape(1, width), attended, gate_in)
    return (normed_output, final_states.reshape(1, heads, E, E))


def solution(mesh):
    placed = (
        P("ctx", "head"),
        P("ctx", "head"),
        P("ctx", "head"),
        P("ctx", "head"),
        P("head"),
        P("head"),
        P(),
        P(),
    )
    return jax.shard_map(
        per_device,
        mesh=mesh,
        in_specs=placed,
        out_specs=(P("ctx", "head"), P("ctx", "head", None, None)),
        check_vma=False,
    )
```

profile of v0, /device:TPU:1, one launch (start us, length us, event | category | flops | bytes accessed | tf_op | source)
XLA Modules:
  0.0 84.7 jit_solution(11633402594603666218)
XLA Ops:
  0.6 0.0 copy-start.4
  0.6 0.0 copy-start.6
  0.7 0.0 copy-start.8
  0.7 6.7 %states.1 = (bf16[32,3,32,128]{3,2,1,0:T(8,128)(2,1)}, f32[8,128,128]{2,1,0:T(8,128)}) custom-call(s32[32]{0:T(128)} %starts_hbm.3, f32[8]{0:T(128)} %rates_hbm.3, bf16[1024,1024]{1,0:T(8,128)(2,1)} %k_hbm.3, bf16[1024,1024]{1,0:T(8,128)(2,1)} %v_hbm.3), custom_call_target="tpu_custom_call" | custom-call | flops 805306368 | bytes 5242880 | tf_op jit(solution)/shard_map/states/pallas_call | solution.py:386
  7.3 31.1 %all_to_all.15.got_ref = bf16[32,3,32,128]{3,2,1,0:T(8,128)(2,1)S(1)} all-to-all(bf16[32,3,32,128]{3,2,1,0:T(8,128)(2,1)} %get-tuple-element.9), channel_id=1, replica_groups=mesh['ctx'=32,'head'=8] {'ctx'}, dimensions={0} | all-to-all | bytes 1572864 | tf_op jit(solution)/shard_map/all_to_all | solution.py:366
  38.4 0.0 copy-done.4
  38.5 0.0 copy-done.6
  38.5 0.0 copy-done.8
  38.5 1.8 %scan.1 = bf16[32,2,32,128]{3,2,1,0:T(8,128)(2,1)} custom-call(s32[32]{0:T(128)S(1)} %copy-done.4, s32[32]{0:T(128)S(1)} %copy-done.8, f32[8]{0:T(128)S(1)} %copy-done.6, bf16[32,3,32,128]{3,2,1,0:T(8,128)(2,1)S(1)} %all_to_all.15.got_ref), custom_call_target="tpu_custom_call" | custom-call | flops 1048576 | bytes 2097152 | tf_op jit(solution)/shard_map/scan/pallas_call | solution.py:437
  40.3 8.4 %all-to-all-start.1 = ((bf16[32,2,32,128]{3,2,1,0:T(8,128)(2,1)}), bf16[32,2,32,128]{3,2,1,0:T(8,128)(2,1)S(1)}, u32[]{:S(2)}, u32[]{:S(2)}) async-start(bf16[32,2,32,128]{3,2,1,0:T(8,128)(2,1)} %scan.1), calls=%async_computation.1 | async-start | bytes 1048576 | tf_op jit(solution)/shard_map/all_to_all | solution.py:366
  48.7 0.0 copy-start.2
  48.7 0.0 copy-start.5
  48.7 0.0 copy-start.7
  48.7 11.1 %inner.1 = (f32[1024,1024]{1,0:T(8,128)}, bf16[1024,1024]{1,0:T(8,128)(2,1)}) custom-call(s32[32]{0:T(128)} %starts_hbm.3, f32[8]{0:T(128)} %rates_hbm.3, bf16[1024,1024]{1,0:T(8,128)(2,1)} %q_hbm.1, bf16[1024,1024]{1,0:T(8,128)(2,1)} %k_hbm.3, bf16[1024,1024]{1,0:T(8,128)(2,1)} %v_hbm.3), custom_call_target="tpu_custom_call" | custom-call | flops 2147483648 | bytes 12582912 | tf_op jit(solution)/shard_map/inner/pallas_call | solution.py:414
  59.8 2.6 %all-to-all-done.1.back_hbm = bf16[32,2,32,128]{3,2,1,0:T(8,128)(2,1)S(1)} async-done(((bf16[32,2,32,128]{3,2,1,0:T(8,128)(2,1)}), bf16[32,2,32,128]{3,2,1,0:T(8,128)(2,1)S(1)}, u32[]{:S(2)}, u32[]{:S(2)}) %all-to-all-start.1) | async-done | bytes 524320 | tf_op jit(solution)/shard_map/all_to_all | solution.py:366
  62.4 0.0 copy-done.2
  62.4 0.0 copy-done.5
  62.4 0.0 copy-done.7
  62.4 0.0 copy-start.1
  62.4 1.6 %copy-done.1 = bf16[1024,1024]{1,0:T(8,128)(2,1)S(1)} copy-done((bf16[1024,1024]{1,0:T(8,128)(2,1)S(1)}, bf16[1024,1024]{1,0:T(8,128)(2,1)}, u32[]{:S(2)}) %copy-start.1) | copy-done | bytes 2097176
  64.0 0.0 copy-start
  64.0 0.0 copy-start.3
  64.0 4.5 %outer.1 = (f32[1024,1024]{1,0:T(8,128)S(1)}, bf16[32,32,128]{2,1,0:T(8,128)(2,1)}, f32[8,8,128]{2,1,0:T(8,128)S(1)}) custom-call(s32[32]{0:T(128)S(1)} %copy-done.5, f32[8]{0:T(128)S(1)} %copy-done.7, bf16[32,2,32,128]{3,2,1,0:T(8,128)(2,1)S(1)} %all-to-all-done.1.back_hbm, f32[8,128,128]{2,1,0:T(8,128)S(1)} %copy-done.2, bf16[1024,1024]{1,0:T(8,128)(2,1)S(1)} %copy-done.1, ...), custom_call_target="tpu_custom_call" | custom-call | flops 268435456 | bytes 10485760 | tf_op jit(solution)/shard_map/outer/pallas_call | solution.py:450
  68.5 13.5 %all_to_all.16.squares_ref = f32[8,8,128]{2,1,0:T(8,128)S(1)} all-to-all(f32[8,8,128]{2,1,0:T(8,128)S(1)} %get-tuple-element.13), channel_id=1, replica_groups=mesh['ctx'=32,'head'=8] {'head'}, dimensions={0} | all-to-all | bytes 65536 | tf_op jit(solution)/shard_map/all_to_all | solution.py:366
  82.0 0.0 copy-done
  82.0 0.0 copy-done.3
  82.0 2.6 %norm.1 = bf16[1024,1024]{1,0:T(8,128)(2,1)} custom-call(f32[8,8,128]{2,1,0:T(8,128)S(1)} %all_to_all.16.squares_ref, f32[1,1024]{1,0:T(1,128)S(1)} %bitcast.2, f32[1024,1024]{1,0:T(8,128)S(1)} %get-tuple-element.14.att_ref, bf16[1024,1024]{1,0:T(8,128)(2,1)S(1)} %copy-done), custom_call_target="tpu_custom_call" | custom-call | flops 6291456 | bytes 8388608 | tf_op jit(solution)/shard_map/norm/pallas_call | solution.py:477
Async XLA Ops:
  0.6 37.8 %copy-start.4 = (s32[32]{0:T(128)S(1)}, s32[32]{0:T(128)}, u32[]{:S(2)}) copy-start(s32[32]{0:T(128)} %starts_hbm.3) | copy-start | bytes 388
  0.6 37.8 %copy-start.6 = (f32[8]{0:T(128)S(1)}, f32[8]{0:T(128)}, u32[]{:S(2)}) copy-start(f32[8]{0:T(128)} %rates_hbm.3) | copy-start | bytes 100
  0.7 37.8 %copy-start.8 = (s32[32]{0:T(128)S(1)}, s32[32]{0:T(128)}, u32[]{:S(2)}) copy-start(s32[32]{0:T(128)} %slots_ref.1) | copy-start | bytes 388
  40.3 22.1 %all-to-all-start.1 = ((bf16[32,2,32,128]{3,2,1,0:T(8,128)(2,1)}), bf16[32,2,32,128]{3,2,1,0:T(8,128)(2,1)S(1)}, u32[]{:S(2)}, u32[]{:S(2)}) async-start(bf16[32,2,32,128]{3,2,1,0:T(8,128)(2,1)} %scan.1), calls=%async_computation.1 | async-start | bytes 1048576 | tf_op jit(solution)/shard_map/all_to_all | solution.py:366
  48.7 13.7 %copy-start.2 = (f32[8,128,128]{2,1,0:T(8,128)S(1)}, f32[8,128,128]{2,1,0:T(8,128)}, u32[]{:S(2)}) copy-start(f32[8,128,128]{2,1,0:T(8,128)} %get-tuple-element.10.mid_hbm) | copy-start | bytes 1572868
  48.7 13.7 %copy-start.5 = (s32[32]{0:T(128)S(1)}, s32[32]{0:T(128)}, u32[]{:S(2)}) copy-start(s32[32]{0:T(128)} %starts_hbm.3) | copy-start | bytes 388
  48.7 13.7 %copy-start.7 = (f32[8]{0:T(128)S(1)}, f32[8]{0:T(128)}, u32[]{:S(2)}) copy-start(f32[8]{0:T(128)} %rates_hbm.3) | copy-start | bytes 100
  62.4 1.6 %copy-start.1 = (bf16[1024,1024]{1,0:T(8,128)(2,1)S(1)}, bf16[1024,1024]{1,0:T(8,128)(2,1)}, u32[]{:S(2)}) copy-start(bf16[1024,1024]{1,0:T(8,128)(2,1)} %get-tuple-element.11.act_hbm) | copy-start | bytes 6291460
  64.0 18.0 %copy-start = (bf16[1024,1024]{1,0:T(8,128)(2,1)S(1)}, bf16[1024,1024]{1,0:T(8,128)(2,1)}, u32[]{:S(2)}) copy-start(bf16[1024,1024]{1,0:T(8,128)(2,1)} %gate_hbm.1) | copy-start | bytes 6291460
  64.0 18.0 %copy-start.3 = (f32[1024]{0:T(1024)S(1)}, f32[1024]{0:T(1024)}, u32[]{:S(2)}) copy-start(f32[1024]{0:T(1024)} %param.12) | copy-start | bytes 12292
where the time goes:
time: 85 us; the launch traced here: 84.7 us
  blocking collectives  44.6 us (52%)
  Pallas kernels  26.7 us (31%)
  starting transfers between devices  8.37 us (10%)
  waiting for transfers between devices  2.6 us (3%)
  local copies, waits for them, and re-layouts  1.63 us (2%)
    all_to_all x2, blocking collectives, swap(): return lax.all_to_all(array, axis, split_axis=0, concat_axis=0, tiled=True)  44.6 us
    pallas_call x1, Pallas kernels, local(): pl.pallas_call(functools.partial(inner_kernel, rows, ranks), out_shape=(j...  11.1 us
    all_to_all x1, starting transfers between devices, swap(): return lax.all_to_all(array, axis, split_axis=0, concat_axis=0, tiled=True)  8.37 us
    pallas_call x1, Pallas kernels, local(): pl.pallas_call(functools.partial(states_kernel, rows, ranks), out_shape=(...  6.65 us
    pallas_call x1, Pallas kernels, local(): pl.pallas_call(functools.partial(outer_kernel, rows, ranks), out_shape=(j...  4.49 us
    pallas_call x1, Pallas kernels, local(): pl.pallas_call(functools.partial(norm_kernel, float(width * groups)), out...  2.6 us
    all_to_all x1, waiting for transfers between devices, swap(): return lax.all_to_all(array, axis, split_axis=0, concat_axis=0, tiled=True)  2.6 us
    pallas_call x1, Pallas kernels, local(): pl.pallas_call(functools.partial(scan_kernel, rows), out_shape=jax.ShapeD...  1.83 us
  transfers between devices with their start and end apart: 1, of which 1 were waited for; matrix products, arithmetic and copies ran while one was open for 0% of the time, Pallas kernels for 13%

commit v1 on v0

--- a/solution.py
+++ b/solution.py
@@ -18,7 +18,7 @@
 norm_eps = 1e-06
 MIB = 1 << 20
 LIMIT = 62 * MIB
-ROOM = 44 * MIB
+ROOM = 40 * MIB
 f32 = jnp.float32
 bf16 = jnp.bfloat16
 SMEM = pl.BlockSpec(memory_space=pltpu.SMEM)
@@ -178,7 +178,7 @@
 
 
 def scan_kernel(
-    rows, starts_ref, slots_ref, rates_ref, got_ref, back_ref, counts, carried
+    rows, starts_ref, slots_ref, rates_ref, got_ref, inner_hbm, back_ref, counts, carried
 ):
     ranks = got_ref.shape[0]
     rate = my_rate(rates_ref, ranks)
@@ -264,34 +264,12 @@
 
 
 def outer_kernel(
-    rows, ranks, starts_hbm, rates_hbm, back_hbm, mid_hbm, act_hbm, inner_hbm,
-    out_ref, final_hbm, squares_ref,
-    starts_ref, rates_ref, back, mid, act, inner, total, arrived, left,
-):
-    heads = mid.shape[0]
-    share = back.shape[0] // heads
-
-    def load(head):
-        at = lanes(head)
-        return (
-            pltpu.make_async_copy(act_hbm.at[:, at], act.at[:, at], arrived.at[0, head]),
-            pltpu.make_async_copy(inner_hbm.at[:, at], inner.at[:, at], arrived.at[1, head]),
-        )
-
-    whole = (
-        pltpu.make_async_copy(starts_hbm, starts_ref, arrived.at[0, heads + 1]),
-        pltpu.make_async_copy(rates_hbm, rates_ref, arrived.at[1, heads + 1]),
-        pltpu.make_async_copy(back_hbm, back, arrived.at[0, heads]),
-        pltpu.make_async_copy(mid_hbm, mid, arrived.at[1, heads]),
-    )
-    finals = pltpu.make_async_copy(back.at[:, 1], final_hbm, left.at[0])
-    for copy in whole:
-        copy.start()
-    for head in range(heads):
-        for copy in load(head):
-            copy.start()
-    for copy in whole:
-        copy.wait()
+    rows, ranks, starts_ref, rates_ref, back_ref, mid_ref, act_ref, inner_ref,
+    out_ref, final_hbm, squares_ref, total, left,
+):
+    heads = mid_ref.shape[0]
+    share = back_ref.shape[0] // heads
+    finals = pltpu.make_async_copy(back_ref.at[:, 1], final_hbm, left.at[0])
     finals.start()
     end_a, end_b = local_ends(starts_ref, rows, ranks)
     mid_end = jnp.where(end_a >= BLOCK - 1, end_a, jnp.where(end_b >= BLOCK - 1, end_b, ABSENT))
@@ -302,17 +280,17 @@
     def _(head):
         at = lanes(head)
         power = power_of(rates_ref, head)
-        incoming = back[pl.ds(head * share, share), 0].reshape(E, E)
-        later = mid[head] + incoming.astype(f32) * (scalar_exp2(float(BLOCK) * power) * from_before)
+        incoming = back_ref[pl.ds(head * share, share), 0].reshape(E, E)
+        later = mid_ref[head] + incoming.astype(f32) * (
+            scalar_exp2(float(BLOCK) * power) * from_before
+        )
         steps = lax.broadcasted_iota(jnp.int32, (BLOCK, E), 0)
         reach = jnp.exp2((steps + 1).astype(f32) * power)
-        for copy in load(head):
-            copy.wait()
         for block, (state, last) in enumerate(((incoming, end_a), (later.astype(bf16), mid_end))):
             span = pl.ds(block * BLOCK, BLOCK)
-            outer = jnp.dot(act[span, at], state, preferred_element_type=f32)
+            outer = jnp.dot(act_ref[span, at], state, preferred_element_type=f32)
             lead = jnp.where(steps + block * BLOCK <= last, reach, 0.0)
-            attended = inner[span, at] + outer * lead
+            attended = inner_ref[span, at] + outer * lead
             out_ref[span, at] = attended
             total[span, :] += attended * attended
 
@@ -328,29 +306,22 @@
 
 
 def norm_kernel(
-    features, squares_ref, gain_ref, att_ref, gate_hbm, out_hbm, gate, out, sems
+    features, squares_ref, gain_ref, att_ref, gate_ref, out_hbm, out, sems
 ):
     bands = out.shape[0] // E
-
-    def load(band):
-        span = pl.ds(band * E, E)
-        return pltpu.make_async_copy(gate_hbm.at[span, :], gate.at[span, :], sems.at[0, band])
 
     def store(band):
         span = pl.ds(band * E, E)
-        return pltpu.make_async_copy(out.at[span, :], out_hbm.at[span, :], sems.at[1, band])
-
-    for band in range(bands):
-        load(band).start()
+        return pltpu.make_async_copy(out.at[span, :], out_hbm.at[span, :], sems.at[band])
+
     total = jnp.sum(squares_ref[...], axis=0)
     scale = lax.rsqrt(total * (1.0 / features) + norm_eps)
     for band in range(bands):
         span = pl.ds(band * E, E)
         column = jnp.broadcast_to(scale[band : band + 1], (E, E)).T
-        load(band).wait()
         for first in range(0, out.shape[1], E):
             cols = slice(first, first + E)
-            opened = 0.5 + 0.5 * jnp.tanh(0.5 * gate[span, cols].astype(f32))
+            opened = 0.5 + 0.5 * jnp.tanh(0.5 * gate_ref[span, cols].astype(f32))
             scaled = att_ref[span, cols] * column * gain_ref[:, cols]
             out[span, cols] = (scaled * opened).astype(bf16)
         store(band).start()
@@ -437,13 +408,13 @@
     back = pl.pallas_call(
         functools.partial(scan_kernel, rows),
         out_shape=jax.ShapeDtypeStruct((ranks, 2, piece, E), bf16),
-        in_specs=[SMEM, SMEM, SMEM, VMEM],
+        in_specs=[SMEM, SMEM, SMEM, VMEM, HBM],
         out_specs=VMEM,
         scratch_shapes=[pltpu.SMEM((ranks,), jnp.int32), pltpu.VMEM((ranks, piece, E), f32)],
-        compiler_params=pltpu.CompilerParams(vmem_limit_bytes=8 * MIB),
+        compiler_params=pltpu.CompilerParams(vmem_limit_bytes=50 * MIB),
         cost_estimate=cost(MIB, 2 * MIB, 0),
         name="scan",
-    )(request_starts, request_slots, decay_rate, got)
+    )(request_starts, request_slots, decay_rate, got, inner)
 
     returned = swap(back, "ctx")
 
@@ -454,19 +425,10 @@
             jax.ShapeDtypeStruct((ranks, piece, E), bf16),
             jax.ShapeDtypeStruct((groups, rows // E, E), f32),
         ),
-        in_specs=[HBM] * 6,
+        in_specs=[SMEM, SMEM, VMEM, VMEM, VMEM, VMEM],
         out_specs=(VMEM, HBM, VMEM),
-        scratch_shapes=[
-            pltpu.SMEM(request_starts.shape, jnp.int32),
-            pltpu.SMEM(decay_rate.shape, f32),
-            pltpu.VMEM((ranks, 2, piece, E), bf16),
-            pltpu.VMEM((heads, E, E), f32),
-            pltpu.VMEM((rows, width), bf16),
-            pltpu.VMEM((rows, width), f32),
-            pltpu.VMEM((rows, E), f32),
-            pltpu.SemaphoreType.DMA((2, heads + 2)),
-            pltpu.SemaphoreType.DMA((1,)),
-        ],
+        scratch_shapes=[pltpu.VMEM((rows, E), f32), pltpu.SemaphoreType.DMA((1,))],
+        input_output_aliases={5: 0},
         compiler_params=pltpu.CompilerParams(vmem_limit_bytes=ROOM),
         cost_estimate=cost(2 * rows * width * E, 10 * MIB, MIB),
         name="outer",
@@ -477,12 +439,11 @@
     normed_output = pl.pallas_call(
         functools.partial(norm_kernel, float(width * groups)),
         out_shape=jax.ShapeDtypeStruct((rows, width), bf16),
-        in_specs=[VMEM, VMEM, VMEM, HBM],
+        in_specs=[VMEM, VMEM, VMEM, VMEM],
         out_specs=HBM,
         scratch_shapes=[
             pltpu.VMEM((rows, width), bf16),
-            pltpu.VMEM((rows, width), bf16),
-            pltpu.SemaphoreType.DMA((2, rows // E)),
+            pltpu.SemaphoreType.DMA((rows // E,)),
         ],
         compiler_params=pltpu.CompilerParams(vmem_limit_bytes=ROOM),
         cost_estimate=cost(6 * rows * width, 8 * MIB, rows * width),

time: 85 us -> 81.2 us (0.955)
  blocking collectives: 44.6 us -> 35.7 us
  waiting for transfers between devices: 2.6 us -> 8.09 us
  starting transfers between devices: 8.37 us -> 11.9 us
  Pallas kernels: 26.7 us -> 24.5 us
  local copies, waits for them, and re-layouts: 1.63 us -> 0.05 us
    all_to_all x2, blocking collectives: 44.6 us -> 35.7 us  [swap(): return lax.all_to_all(array, axis, split_axis=0, concat_axis=0, tiled=True)]
    all_to_all x1, waiting for transfers between devices: 2.6 us -> 8.09 us  [swap(): return lax.all_to_all(array, axis, split_axis=0, concat_axis=0, tiled=True)]
    all_to_all x1, starting transfers between devices: 8.37 us -> 11.9 us  [swap(): return lax.all_to_all(array, axis, split_axis=0, concat_axis=0, tiled=True)]
    unnamed x18 -> x16, local copies, waits for them, and re-layouts: 1.63 us -> 0.05 us
    pallas_call x1, Pallas kernels: 4.49 us -> 3.49 us  [local(): pl.pallas_call(functools.partial(outer_kernel, rows, ranks), out_shape=(j...]
  transfers between devices with their start and end apart: 1 -> 1, of which waited for: 1 -> 1; matrix products, arithmetic and copies ran while one was open for 0% -> 0% of each run, Pallas kernels for 13% -> 14%
where the time goes in v1:
time: 81.2 us; the launch traced here: 80.9 us
  blocking collectives  35.7 us (44%)
  Pallas kernels  24.5 us (30%)
  starting transfers between devices  11.9 us (15%)
  waiting for transfers between devices  8.09 us (10%)
    all_to_all x2, blocking collectives, swap(): return lax.all_to_all(array, axis, split_axis=0, concat_axis=0, tiled=True)  35.7 us
    all_to_all x1, starting transfers between devices, swap(): return lax.all_to_all(array, axis, split_axis=0, concat_axis=0, tiled=True)  11.9 us
    pallas_call x1, Pallas kernels, local(): pl.pallas_call(functools.partial(inner_kernel, rows, ranks), out_shape=(j...  11.1 us
    all_to_all x1, waiting for transfers between devices, swap(): return lax.all_to_all(array, axis, split_axis=0, concat_axis=0, tiled=True)  8.09 us
    pallas_call x1, Pallas kernels, local(): pl.pallas_call(functools.partial(states_kernel, rows, ranks), out_shape=(...  6.68 us
    pallas_call x1, Pallas kernels, local(): pl.pallas_call(functools.partial(outer_kernel, rows, ranks), out_shape=(j...  3.49 us
    pallas_call x1, Pallas kernels, local(): pl.pallas_call(functools.partial(norm_kernel, float(width * groups)), out...  2.17 us
  transfers between devices with their start and end apart: 1, of which 1 were waited for; matrix products, arithmetic and copies ran while one was open for 0% of the time, Pallas kernels for 14%

profile of v1, /device:TPU:1, one launch (start us, length us, event | category | flops | bytes accessed | tf_op | source)
XLA Modules:
  0.0 80.9 jit_solution(16838747061105937498)
XLA Ops:
  0.6 6.7 %states.1 = (bf16[32,3,32,128]{3,2,1,0:T(8,128)(2,1)}, f32[8,128,128]{2,1,0:T(8,128)}) custom-call(s32[32]{0:T(128)} %starts_ref.5, f32[8]{0:T(128)} %rates_ref.5, bf16[1024,1024]{1,0:T(8,128)(2,1)} %k_hbm.3, bf16[1024,1024]{1,0:T(8,128)(2,1)} %v_hbm.3), custom_call_target="tpu_custom_call" | custom-call | flops 805306368 | bytes 5242880 | tf_op jit(solution)/shard_map/states/pallas_call | solution.py:357
  7.3 11.9 %all-to-all-start = ((bf16[32,3,32,128]{3,2,1,0:T(8,128)(2,1)}), bf16[32,3,32,128]{3,2,1,0:T(8,128)(2,1)S(1)}, u32[]{:S(2)}, u32[]{:S(2)}) async-start(bf16[32,3,32,128]{3,2,1,0:T(8,128)(2,1)} %get-tuple-element.9), calls=%async_computation | async-start | bytes 1572864 | tf_op jit(solution)/shard_map/all_to_all | solution.py:337
  19.2 0.0 copy-start.5
  19.2 0.0 copy-start.6
  19.2 0.0 copy-start.7
  19.2 0.0 copy-start.3
  19.2 11.1 %inner.1 = (f32[1024,1024]{1,0:T(8,128)}, bf16[1024,1024]{1,0:T(8,128)(2,1)}) custom-call(s32[32]{0:T(128)} %starts_ref.5, f32[8]{0:T(128)} %rates_ref.5, bf16[1024,1024]{1,0:T(8,128)(2,1)} %q_hbm.1, bf16[1024,1024]{1,0:T(8,128)(2,1)} %k_hbm.3, bf16[1024,1024]{1,0:T(8,128)(2,1)} %v_hbm.3), custom_call_target="tpu_custom_call" | custom-call | flops 2147483648 | bytes 12582912 | tf_op jit(solution)/shard_map/inner/pallas_call | solution.py:385
  30.4 8.1 %all-to-all-done.got_ref = bf16[32,3,32,128]{3,2,1,0:T(8,128)(2,1)S(1)} async-done(((bf16[32,3,32,128]{3,2,1,0:T(8,128)(2,1)}), bf16[32,3,32,128]{3,2,1,0:T(8,128)(2,1)S(1)}, u32[]{:S(2)}, u32[]{:S(2)}) %all-to-all-start) | async-done | bytes 786464 | tf_op jit(solution)/shard_map/all_to_all | solution.py:337
  38.4 0.0 copy-done.5
  38.4 0.0 copy-done.6
  38.4 0.0 copy-done.7
  38.5 0.0 copy-start
  38.5 0.0 copy-start.2
  38.5 1.0 %scan.1 = bf16[32,2,32,128]{3,2,1,0:T(8,128)(2,1)S(1)} custom-call(s32[32]{0:T(128)S(1)} %copy-done.5, s32[32]{0:T(128)S(1)} %copy-done.7, f32[8]{0:T(128)S(1)} %copy-done.6, bf16[32,3,32,128]{3,2,1,0:T(8,128)(2,1)S(1)} %all-to-all-done.got_ref, f32[1024,1024]{1,0:T(8,128)} %get-tuple-element.10.inner_hbm.inner_ref), custom_call_target="tpu_custom_call" | custom-call | flops 1048576 | bytes 2097152 | tf_op jit(solution)/shard_map/scan/pallas_call | solution.py:408
  39.5 22.2 %all_to_all.15.back_ref = bf16[32,2,32,128]{3,2,1,0:T(8,128)(2,1)S(1)} all-to-all(bf16[32,2,32,128]{3,2,1,0:T(8,128)(2,1)S(1)} %scan.1), channel_id=1, replica_groups=mesh['ctx'=32,'head'=8] {'ctx'}, dimensions={0} | all-to-all | bytes 1048576 | tf_op jit(solution)/shard_map/all_to_all | solution.py:337
  61.7 0.0 copy-done.3
  61.7 0.0 copy-done
  61.7 0.0 copy-done.2
  61.7 0.0 copy-start.1
  61.7 0.0 copy-start.4
  61.7 3.5 %outer.1 = (f32[1024,1024]{1,0:T(8,128)S(1)}, bf16[32,32,128]{2,1,0:T(8,128)(2,1)}, f32[8,8,128]{2,1,0:T(8,128)S(1)}) custom-call(s32[32]{0:T(128)S(1)} %copy-done.5, f32[8]{0:T(128)S(1)} %copy-done.6, bf16[32,2,32,128]{3,2,1,0:T(8,128)(2,1)S(1)} %all_to_all.15.back_ref, f32[8,128,128]{2,1,0:T(8,128)S(1)} %copy-done.3, ...), custom_call_target="tpu_custom_call", output_to_operand_aliasing={{0}: (5, {})} | custom-call | flops 268435456 | bytes 10485760 | tf_op jit(solution)/shard_map/outer/pallas_call | solution.py:421
  65.2 13.5 %all_to_all.16.squares_ref = f32[8,8,128]{2,1,0:T(8,128)S(1)} all-to-all(f32[8,8,128]{2,1,0:T(8,128)S(1)} %get-tuple-element.13), channel_id=1, replica_groups=mesh['ctx'=32,'head'=8] {'head'}, dimensions={0} | all-to-all | bytes 65536 | tf_op jit(solution)/shard_map/all_to_all | solution.py:337
  78.8 0.0 copy-done.1
  78.8 0.0 copy-done.4
  78.8 2.2 %norm.1 = bf16[1024,1024]{1,0:T(8,128)(2,1)} custom-call(f32[8,8,128]{2,1,0:T(8,128)S(1)} %all_to_all.16.squares_ref, f32[1,1024]{1,0:T(1,128)S(1)} %bitcast.2, f32[1024,1024]{1,0:T(8,128)S(1)} %get-tuple-element.14.att_ref, bf16[1024,1024]{1,0:T(8,128)(2,1)S(1)} %copy-done.1), custom_call_target="tpu_custom_call" | custom-call | flops 6291456 | bytes 8388608 | tf_op jit(solution)/shard_map/norm/pallas_call | solution.py:439
Async XLA Ops:
  7.3 31.1 %all-to-all-start = ((bf16[32,3,32,128]{3,2,1,0:T(8,128)(2,1)}), bf16[32,3,32,128]{3,2,1,0:T(8,128)(2,1)S(1)}, u32[]{:S(2)}, u32[]{:S(2)}) async-start(bf16[32,3,32,128]{3,2,1,0:T(8,128)(2,1)} %get-tuple-element.9), calls=%async_computation | async-start | bytes 1572864 | tf_op jit(solution)/shard_map/all_to_all | solution.py:337
  19.2 19.2 %copy-start.5 = (s32[32]{0:T(128)S(1)}, s32[32]{0:T(128)}, u32[]{:S(2)}) copy-start(s32[32]{0:T(128)} %starts_ref.5) | copy-start | bytes 388
  19.2 19.2 %copy-start.6 = (f32[8]{0:T(128)S(1)}, f32[8]{0:T(128)}, u32[]{:S(2)}) copy-start(f32[8]{0:T(128)} %rates_ref.5) | copy-start | bytes 100
  19.2 19.2 %copy-start.7 = (s32[32]{0:T(128)S(1)}, s32[32]{0:T(128)}, u32[]{:S(2)}) copy-start(s32[32]{0:T(128)} %slots_ref.1) | copy-start | bytes 388
  19.2 42.5 %copy-start.3 = (f32[8,128,128]{2,1,0:T(8,128)S(1)}, f32[8,128,128]{2,1,0:T(8,128)}, u32[]{:S(2)}) copy-start(f32[8,128,128]{2,1,0:T(8,128)} %get-tuple-element.11.mid_ref) | copy-start | bytes 1572868
  38.5 23.3 %copy-start = (f32[1024,1024]{1,0:T(8,128)S(1)}, f32[1024,1024]{1,0:T(8,128)}, u32[]{:S(2)}) copy-start(f32[1024,1024]{1,0:T(8,128)} %get-tuple-element.10.inner_hbm.inner_ref) | copy-start | bytes 12582916
  38.5 23.2 %copy-start.2 = (bf16[1024,1024]{1,0:T(8,128)(2,1)S(1)}, bf16[1024,1024]{1,0:T(8,128)(2,1)}, u32[]{:S(2)}) copy-start(bf16[1024,1024]{1,0:T(8,128)(2,1)} %get-tuple-element.12.act_ref) | copy-start | bytes 6291460
  61.7 17.1 %copy-start.1 = (bf16[1024,1024]{1,0:T(8,128)(2,1)S(1)}, bf16[1024,1024]{1,0:T(8,128)(2,1)}, u32[]{:S(2)}) copy-start(bf16[1024,1024]{1,0:T(8,128)(2,1)} %gate_ref.1) | copy-start | bytes 6291460
  61.7 17.0 %copy-start.4 = (f32[1024]{0:T(1024)S(1)}, f32[1024]{0:T(1024)}, u32[]{:S(2)}) copy-start(f32[1024]{0:T(1024)} %param.12) | copy-start | bytes 12292

commit v2 on v1

--- a/solution.py
+++ b/solution.py
@@ -26,9 +26,13 @@
 HBM = pl.BlockSpec(memory_space=pltpu.HBM)
 
 
+def silu_wide(values):
+    half = values.astype(f32) * 0.5
+    return half + half * jnp.tanh(half)
+
+
 def silu(values):
-    half = values.astype(f32) * 0.5
-    return (half + half * jnp.tanh(half)).astype(bf16)
+    return silu_wide(values).astype(bf16)
 
 
 def rate_of(rates_ref, head):
@@ -72,7 +76,7 @@
 
 def states_kernel(
     rows, ranks, starts_hbm, rates_hbm, k_hbm, v_hbm, sums_hbm, mid_hbm,
-    starts_ref, rates_ref, k_raw, v_raw, gap, masks, sums, mids, sems, arrived, left,
+    starts_ref, rates_ref, k_raw, v_raw, gap, upto, sums, mids, sems, arrived, left,
 ):
     heads = k_raw.shape[1] // E
     small = (
@@ -107,43 +111,55 @@
     token = lax.broadcasted_iota(jnp.int32, (rows, E), 0)
     in_a = token <= end_a
     in_b = token <= end_b
-    seg_end = jnp.where(in_a, end_a, jnp.where(in_b, end_b, ABSENT))
-    block_end = (token // BLOCK) * BLOCK + (BLOCK - 1)
-    gap[...] = (jnp.minimum(seg_end, block_end) - token).astype(f32)
-    masks[0] = jnp.where(in_a, 1.0, 0.0).astype(bf16)
-    masks[1] = jnp.where(in_b, jnp.where(in_a, 0.0, 1.0), 0.0).astype(bf16)
-    masks[2] = jnp.where(in_b, 0.0, 1.0).astype(bf16)
+    place = lax.broadcasted_iota(jnp.int32, (8, rows), 1)
+    place_end = jnp.where(place <= end_a, end_a, jnp.where(place <= end_b, end_b, ABSENT))
+    last = (place // BLOCK) * BLOCK + (BLOCK - 1)
+    gap[...] = (jnp.minimum(place_end, last) - place).astype(f32)
+    upto[0] = jnp.where(in_a, 1.0, 0.0)
+    upto[1] = jnp.where(in_b, 1.0, 0.0)
     at_mid = (end_a < BLOCK - 1).astype(jnp.int32) + (end_b < BLOCK - 1).astype(jnp.int32)
 
-    @pl.loop(0, heads)
-    def _(head):
+    def work(head):
         at = lanes(head)
         power = power_of(rates_ref, head)
-        for copy in load(head):
-            copy.wait()
         parts = []
         for first in range(0, rows, BLOCK):
             span = pl.ds(first, BLOCK)
-            keys = silu(k_raw[span, at])
-            values = silu(v_raw[span, at])
-            scaled = (keys.astype(f32) * jnp.exp2(gap[span, :] * power)).astype(bf16)
-            spread = jnp.concatenate([values * masks[x, span, :] for x in range(SEGS)], axis=1)
-            parts.append(
-                lax.dot_general(
-                    scaled, spread, (((0,), (0,)), ((), ())), preferred_element_type=f32
-                )
+            keys = silu(k_raw[span, at].T)
+            values = silu_wide(v_raw[span, at])
+            decay = jnp.exp2(gap[:, span] * power)
+            scaled = (keys.astype(f32) * decay[:1, :]).astype(bf16)
+            spread = jnp.concatenate(
+                [
+                    (values * upto[0, span, :]).astype(bf16),
+                    (values * upto[1, span, :]).astype(bf16),
+                    values.astype(bf16),
+                ],
+                axis=1,
             )
+            running = jnp.dot(scaled, spread, preferred_element_type=f32)
+            until_a, until_b, until_c = (running[:, x * E : (x + 1) * E] for x in range(SEGS))
+            parts.append((until_a, until_b - until_a, until_c - until_b))
         early, late = parts
         mid = jnp.zeros((E, E), f32)
         for x, end in enumerate((end_a, end_b, jnp.int32(ABSENT))):
             reach = jnp.maximum(jnp.minimum(end, rows - 1) - (BLOCK - 1), 0).astype(f32)
-            cols = slice(x * E, (x + 1) * E)
-            total = early[:, cols] * scalar_exp2(reach * power) + late[:, cols]
+            total = early[x] * scalar_exp2(reach * power) + late[x]
             sums[pl.ds(head * share, share), x] = total.astype(bf16).reshape(share, -1, E)
-            mid += early[:, cols] * (at_mid == x).astype(f32)
+            mid += early[x] * (at_mid == x).astype(f32)
         mids[head] = mid
-        for copy in store(head):
-            copy.start()
+
+    @pl.loop(0, heads // 2)
+    def _(group):
+        mine = [group * 2 + index for index in range(2)]
+        for head in mine:
+            for copy in load(head):
+                copy.wait()
+        for head in mine:
+            work(head)
+        for head in mine:
+            for copy in store(head):
+                copy.start()
 
     for head in range(heads):
         for copy in store(head):
@@ -265,7 +281,7 @@
 
 def outer_kernel(
     rows, ranks, starts_ref, rates_ref, back_ref, mid_ref, act_ref, inner_ref,
-    out_ref, final_hbm, squares_ref, total, left,
+    out_ref, final_hbm, squares_ref, total, lead, left,
 ):
     heads = mid_ref.shape[0]
     share = back_ref.shape[0] // heads
@@ -275,8 +291,12 @@
     mid_end = jnp.where(end_a >= BLOCK - 1, end_a, jnp.where(end_b >= BLOCK - 1, end_b, ABSENT))
     from_before = (end_a >= BLOCK - 1).astype(f32)
     total[...] = jnp.zeros_like(total)
-
-    @pl.loop(0, heads)
+    steps = lax.broadcasted_iota(jnp.int32, (BLOCK, E), 0)
+    for block, last in enumerate((end_a, mid_end)):
+        here = steps + block * BLOCK <= last
+        lead[block] = jnp.where(here, (steps + 1).astype(f32), FAR)
+
+    @pl.loop(0, heads, unroll=4)
     def _(head):
         at = lanes(head)
         power = power_of(rates_ref, head)
@@ -284,13 +304,10 @@
         later = mid_ref[head] + incoming.astype(f32) * (
             scalar_exp2(float(BLOCK) * power) * from_before
         )
-        steps = lax.broadcasted_iota(jnp.int32, (BLOCK, E), 0)
-        reach = jnp.exp2((steps + 1).astype(f32) * power)
-        for block, (state, last) in enumerate(((incoming, end_a), (later.astype(bf16), mid_end))):
+        for block, state in enumerate((incoming, later.astype(bf16))):
             span = pl.ds(block * BLOCK, BLOCK)
             outer = jnp.dot(act_ref[span, at], state, preferred_element_type=f32)
-            lead = jnp.where(steps + block * BLOCK <= last, reach, 0.0)
-            attended = inner_ref[span, at] + outer * lead
+            attended = inner_ref[span, at] + outer * jnp.exp2(lead[block] * power)
             out_ref[span, at] = attended
             total[span, :] += attended * attended
 
@@ -315,13 +332,13 @@
         return pltpu.make_async_copy(out.at[span, :], out_hbm.at[span, :], sems.at[band])
 
     total = jnp.sum(squares_ref[...], axis=0)
-    scale = lax.rsqrt(total * (1.0 / features) + norm_eps)
+    scale = 0.5 * lax.rsqrt(total * (1.0 / features) + norm_eps)
     for band in range(bands):
         span = pl.ds(band * E, E)
         column = jnp.broadcast_to(scale[band : band + 1], (E, E)).T
         for first in range(0, out.shape[1], E):
             cols = slice(first, first + E)
-            opened = 0.5 + 0.5 * jnp.tanh(0.5 * gate_ref[span, cols].astype(f32))
+            opened = 1.0 + jnp.tanh(0.5 * gate_ref[span, cols].astype(f32))
             scaled = att_ref[span, cols] * column * gain_ref[:, cols]
             out[span, cols] = (scaled * opened).astype(bf16)
         store(band).start()
@@ -367,8 +384,8 @@
             pltpu.SMEM(decay_rate.shape, f32),
             pltpu.VMEM((rows, width), bf16),
             pltpu.VMEM((rows, width), bf16),
-            pltpu.VMEM((rows, E), f32),
-            pltpu.VMEM((SEGS, rows, E), bf16),
+            pltpu.VMEM((8, rows), f32),
+            pltpu.VMEM((ENDS_MOST, rows, E), f32),
             pltpu.VMEM((ranks, SEGS, piece, E), bf16),
             pltpu.VMEM((heads, E, E), f32),
             pltpu.SemaphoreType.DMA((2,)),
@@ -427,7 +444,11 @@
         ),
         in_specs=[SMEM, SMEM, VMEM, VMEM, VMEM, VMEM],
         out_specs=(VMEM, HBM, VMEM),
-        scratch_shapes=[pltpu.VMEM((rows, E), f32), pltpu.SemaphoreType.DMA((1,))],
+        scratch_shapes=[
+            pltpu.VMEM((rows, E), f32),
+            pltpu.VMEM((rows // BLOCK, BLOCK, E), f32),
+            pltpu.SemaphoreType.DMA((1,)),
+        ],
         input_output_aliases={5: 0},
         compiler_params=pltpu.CompilerParams(vmem_limit_bytes=ROOM),
         cost_estimate=cost(2 * rows * width * E, 10 * MIB, MIB),

time: 81.2 us -> 80 us (0.985)
  Pallas kernels: 24.5 us -> 23.3 us
where the time goes in v2:
time: 80 us; the launch traced here: 79.8 us
  blocking collectives  35.7 us (45%)
  Pallas kernels  23.3 us (29%)
  starting transfers between devices  11.9 us (15%)
  waiting for transfers between devices  8.11 us (10%)
    all_to_all x2, blocking collectives, swap(): return lax.all_to_all(array, axis, split_axis=0, concat_axis=0, tiled=True)  35.7 us
    all_to_all x1, starting transfers between devices, swap(): return lax.all_to_all(array, axis, split_axis=0, concat_axis=0, tiled=True)  11.9 us
    pallas_call x1, Pallas kernels, local(): pl.pallas_call(functools.partial(inner_kernel, rows, ranks), out_shape=(j...  11.1 us
    all_to_all x1, waiting for transfers between devices, swap(): return lax.all_to_all(array, axis, split_axis=0, concat_axis=0, tiled=True)  8.11 us
    pallas_call x1, Pallas kernels, local(): pl.pallas_call(functools.partial(states_kernel, rows, ranks), out_shape=(...  5.89 us
    pallas_call x1, Pallas kernels, local(): pl.pallas_call(functools.partial(outer_kernel, rows, ranks), out_shape=(j...  3.22 us
    pallas_call x1, Pallas kernels, local(): pl.pallas_call(functools.partial(norm_kernel, float(width * groups)), out...  2.07 us
  transfers between devices with their start and end apart: 1, of which 1 were waited for; matrix products, arithmetic and copies ran while one was open for 0% of the time, Pallas kernels for 14%

profile of v2, /device:TPU:1, one launch (start us, length us, event | category | flops | bytes accessed | tf_op | source)
XLA Modules:
  0.0 79.8 jit_solution(4683623244474348774)
XLA Ops:
  0.6 5.9 %states.1 = (bf16[32,3,32,128]{3,2,1,0:T(8,128)(2,1)}, f32[8,128,128]{2,1,0:T(8,128)}) custom-call(s32[32]{0:T(128)} %starts_ref.5, f32[8]{0:T(128)} %rates_ref.5, bf16[1024,1024]{1,0:T(8,128)(2,1)} %k_hbm.3, bf16[1024,1024]{1,0:T(8,128)(2,1)} %v_hbm.3), custom_call_target="tpu_custom_call" | custom-call | flops 805306368 | bytes 5242880 | tf_op jit(solution)/shard_map/states/pallas_call | solution.py:374
  6.5 11.9 %all-to-all-start = ((bf16[32,3,32,128]{3,2,1,0:T(8,128)(2,1)}), bf16[32,3,32,128]{3,2,1,0:T(8,128)(2,1)S(1)}, u32[]{:S(2)}, u32[]{:S(2)}) async-start(bf16[32,3,32,128]{3,2,1,0:T(8,128)(2,1)} %get-tuple-element.9), calls=%async_computation | async-start | bytes 1572864 | tf_op jit(solution)/shard_map/all_to_all | solution.py:354
  18.4 0.0 copy-start.5
  18.4 0.0 copy-start.6
  18.4 0.0 copy-start.7
  18.4 0.0 copy-start.3
  18.4 11.1 %inner.1 = (f32[1024,1024]{1,0:T(8,128)}, bf16[1024,1024]{1,0:T(8,128)(2,1)}) custom-call(s32[32]{0:T(128)} %starts_ref.5, f32[8]{0:T(128)} %rates_ref.5, bf16[1024,1024]{1,0:T(8,128)(2,1)} %q_hbm.1, bf16[1024,1024]{1,0:T(8,128)(2,1)} %k_hbm.3, bf16[1024,1024]{1,0:T(8,128)(2,1)} %v_hbm.3), custom_call_target="tpu_custom_call" | custom-call | flops 2147483648 | bytes 12582912 | tf_op jit(solution)/shard_map/inner/pallas_call | solution.py:402
  29.6 8.1 %all-to-all-done.got_ref = bf16[32,3,32,128]{3,2,1,0:T(8,128)(2,1)S(1)} async-done(((bf16[32,3,32,128]{3,2,1,0:T(8,128)(2,1)}), bf16[32,3,32,128]{3,2,1,0:T(8,128)(2,1)S(1)}, u32[]{:S(2)}, u32[]{:S(2)}) %all-to-all-start) | async-done | bytes 786464 | tf_op jit(solution)/shard_map/all_to_all | solution.py:354
  37.7 0.0 copy-done.5
  37.7 0.0 copy-done.6
  37.7 0.0 copy-done.7
  37.7 0.0 copy-start
  37.7 0.0 copy-start.2
  37.7 1.0 %scan.1 = bf16[32,2,32,128]{3,2,1,0:T(8,128)(2,1)S(1)} custom-call(s32[32]{0:T(128)S(1)} %copy-done.5, s32[32]{0:T(128)S(1)} %copy-done.7, f32[8]{0:T(128)S(1)} %copy-done.6, bf16[32,3,32,128]{3,2,1,0:T(8,128)(2,1)S(1)} %all-to-all-done.got_ref, f32[1024,1024]{1,0:T(8,128)} %get-tuple-element.10.inner_hbm.inner_ref), custom_call_target="tpu_custom_call" | custom-call | flops 1048576 | bytes 2097152 | tf_op jit(solution)/shard_map/scan/pallas_call | solution.py:425
  38.7 22.1 %all_to_all.15.back_ref = bf16[32,2,32,128]{3,2,1,0:T(8,128)(2,1)S(1)} all-to-all(bf16[32,2,32,128]{3,2,1,0:T(8,128)(2,1)S(1)} %scan.1), channel_id=1, replica_groups=mesh['ctx'=32,'head'=8] {'ctx'}, dimensions={0} | all-to-all | bytes 1048576 | tf_op jit(solution)/shard_map/all_to_all | solution.py:354
  60.9 0.0 copy-done.3
  60.9 0.0 copy-done
  60.9 0.0 copy-done.2
  60.9 0.0 copy-start.1
  60.9 0.0 copy-start.4
  60.9 3.2 %outer.1 = (f32[1024,1024]{1,0:T(8,128)S(1)}, bf16[32,32,128]{2,1,0:T(8,128)(2,1)}, f32[8,8,128]{2,1,0:T(8,128)S(1)}) custom-call(s32[32]{0:T(128)S(1)} %copy-done.5, f32[8]{0:T(128)S(1)} %copy-done.6, bf16[32,2,32,128]{3,2,1,0:T(8,128)(2,1)S(1)} %all_to_all.15.back_ref, f32[8,128,128]{2,1,0:T(8,128)S(1)} %copy-done.3, ...), custom_call_target="tpu_custom_call", output_to_operand_aliasing={{0}: (5, {})} | custom-call | flops 268435456 | bytes 10485760 | tf_op jit(solution)/shard_map/outer/pallas_call | solution.py:438
  64.2 13.5 %all_to_all.16.squares_ref = f32[8,8,128]{2,1,0:T(8,128)S(1)} all-to-all(f32[8,8,128]{2,1,0:T(8,128)S(1)} %get-tuple-element.13), channel_id=1, replica_groups=mesh['ctx'=32,'head'=8] {'head'}, dimensions={0} | all-to-all | bytes 65536 | tf_op jit(solution)/shard_map/all_to_all | solution.py:354
  77.7 0.0 copy-done.1
  77.7 0.0 copy-done.4
  77.7 2.1 %norm.1 = bf16[1024,1024]{1,0:T(8,128)(2,1)} custom-call(f32[8,8,128]{2,1,0:T(8,128)S(1)} %all_to_all.16.squares_ref, f32[1,1024]{1,0:T(1,128)S(1)} %bitcast.2, f32[1024,1024]{1,0:T(8,128)S(1)} %get-tuple-element.14.att_ref, bf16[1024,1024]{1,0:T(8,128)(2,1)S(1)} %copy-done.1), custom_call_target="tpu_custom_call" | custom-call | flops 6291456 | bytes 8388608 | tf_op jit(solution)/shard_map/norm/pallas_call | solution.py:460
Async XLA Ops:
  6.5 31.1 %all-to-all-start = ((bf16[32,3,32,128]{3,2,1,0:T(8,128)(2,1)}), bf16[32,3,32,128]{3,2,1,0:T(8,128)(2,1)S(1)}, u32[]{:S(2)}, u32[]{:S(2)}) async-start(bf16[32,3,32,128]{3,2,1,0:T(8,128)(2,1)} %get-tuple-element.9), calls=%async_computation | async-start | bytes 1572864 | tf_op jit(solution)/shard_map/all_to_all | solution.py:354
  18.4 19.3 %copy-start.5 = (s32[32]{0:T(128)S(1)}, s32[32]{0:T(128)}, u32[]{:S(2)}) copy-start(s32[32]{0:T(128)} %starts_ref.5) | copy-start | bytes 388
  18.4 19.3 %copy-start.6 = (f32[8]{0:T(128)S(1)}, f32[8]{0:T(128)}, u32[]{:S(2)}) copy-start(f32[8]{0:T(128)} %rates_ref.5) | copy-start | bytes 100
  18.4 19.3 %copy-start.7 = (s32[32]{0:T(128)S(1)}, s32[32]{0:T(128)}, u32[]{:S(2)}) copy-start(s32[32]{0:T(128)} %slots_ref.1) | copy-start | bytes 388
  18.4 42.5 %copy-start.3 = (f32[8,128,128]{2,1,0:T(8,128)S(1)}, f32[8,128,128]{2,1,0:T(8,128)}, u32[]{:S(2)}) copy-start(f32[8,128,128]{2,1,0:T(8,128)} %get-tuple-element.11.mid_ref) | copy-start | bytes 1572868
  37.7 23.2 %copy-start = (f32[1024,1024]{1,0:T(8,128)S(1)}, f32[1024,1024]{1,0:T(8,128)}, u32[]{:S(2)}) copy-start(f32[1024,1024]{1,0:T(8,128)} %get-tuple-element.10.inner_hbm.inner_ref) | copy-start | bytes 12582916
  37.7 23.2 %copy-start.2 = (bf16[1024,1024]{1,0:T(8,128)(2,1)S(1)}, bf16[1024,1024]{1,0:T(8,128)(2,1)}, u32[]{:S(2)}) copy-start(bf16[1024,1024]{1,0:T(8,128)(2,1)} %get-tuple-element.12.act_ref) | copy-start | bytes 6291460
  60.9 16.8 %copy-start.1 = (bf16[1024,1024]{1,0:T(8,128)(2,1)S(1)}, bf16[1024,1024]{1,0:T(8,128)(2,1)}, u32[]{:S(2)}) copy-start(bf16[1024,1024]{1,0:T(8,128)(2,1)} %gate_ref.1) | copy-start | bytes 6291460
  60.9 16.8 %copy-start.4 = (f32[1024]{0:T(1024)S(1)}, f32[1024]{0:T(1024)}, u32[]{:S(2)}) copy-start(f32[1024]{0:T(1024)} %param.12) | copy-start | bytes 12292

commit v3 on v2

--- a/solution.py
+++ b/solution.py
@@ -214,8 +214,9 @@
 
 
 def inner_kernel(
-    rows, ranks, starts_ref, rates_ref, q_hbm, k_hbm, v_hbm, inner_hbm, act_hbm,
-    q_raw, k_raw, v_raw, inner, act, dist, arrived, left,
+    rows, ranks, starts_ref, rates_ref, gain_ref, q_hbm, k_hbm, v_hbm, gate_hbm,
+    inner_hbm, act_hbm, gated_hbm,
+    q_raw, k_raw, v_raw, gate_raw, inner, act, gated, dist, arrived, left,
 ):
     heads = q_raw.shape[1] // E
 
@@ -225,6 +226,7 @@
             pltpu.make_async_copy(q_hbm.at[:, at], q_raw.at[:, at], arrived.at[0, head]),
             pltpu.make_async_copy(k_hbm.at[:, at], k_raw.at[:, at], arrived.at[1, head]),
             pltpu.make_async_copy(v_hbm.at[:, at], v_raw.at[:, at], arrived.at[2, head]),
+            pltpu.make_async_copy(gate_hbm.at[:, at], gate_raw.at[:, at], arrived.at[3, head]),
         )
 
     def store(head):
@@ -232,6 +234,7 @@
         return (
             pltpu.make_async_copy(inner.at[:, at], inner_hbm.at[:, at], left.at[0, head]),
             pltpu.make_async_copy(act.at[:, at], act_hbm.at[:, at], left.at[1, head]),
+            pltpu.make_async_copy(gated.at[:, at], gated_hbm.at[:, at], left.at[2, head]),
         )
 
     for head in range(heads):
@@ -253,6 +256,8 @@
         for copy in load(head):
             copy.wait()
         act[:, at] = silu(q_raw[:, at])
+        opened = 1.0 + jnp.tanh(0.5 * gate_raw[:, at].astype(f32))
+        gated[:, at] = opened * (0.5 * gain_ref[:, at])
         keys = silu(k_raw[:, at])
         values = silu(v_raw[:, at])
         for block in range(rows // BLOCK):
@@ -323,7 +328,7 @@
 
 
 def norm_kernel(
-    features, squares_ref, gain_ref, att_ref, gate_ref, out_hbm, out, sems
+    features, squares_ref, att_ref, gated_ref, out_hbm, out, sems
 ):
     bands = out.shape[0] // E
 
@@ -332,15 +337,13 @@
         return pltpu.make_async_copy(out.at[span, :], out_hbm.at[span, :], sems.at[band])
 
     total = jnp.sum(squares_ref[...], axis=0)
-    scale = 0.5 * lax.rsqrt(total * (1.0 / features) + norm_eps)
+    scale = lax.rsqrt(total * (1.0 / features) + norm_eps)
     for band in range(bands):
         span = pl.ds(band * E, E)
         column = jnp.broadcast_to(scale[band : band + 1], (E, E)).T
         for first in range(0, out.shape[1], E):
             cols = slice(first, first + E)
-            opened = 1.0 + jnp.tanh(0.5 * gate_ref[span, cols].astype(f32))
-            scaled = att_ref[span, cols] * column * gain_ref[:, cols]
-            out[span, cols] = (scaled * opened).astype(bf16)
+            out[span, cols] = (att_ref[span, cols] * column * gated_ref[span, cols]).astype(bf16)
         store(band).start()
     for band in range(bands):
         store(band).wait()
@@ -399,28 +402,31 @@
 
     got = swap(sums, "ctx")
 
-    inner, act = pl.pallas_call(
+    inner, act, gated = pl.pallas_call(
         functools.partial(inner_kernel, rows, ranks),
         out_shape=(
             jax.ShapeDtypeStruct((rows, width), f32),
             jax.ShapeDtypeStruct((rows, width), bf16),
+            jax.ShapeDtypeStruct((rows, width), f32),
         ),
-        in_specs=[SMEM, SMEM, HBM, HBM, HBM],
-        out_specs=(HBM, HBM),
+        in_specs=[SMEM, SMEM, VMEM, HBM, HBM, HBM, HBM],
+        out_specs=(HBM, HBM, HBM),
         scratch_shapes=[
             pltpu.VMEM((rows, width), bf16),
             pltpu.VMEM((rows, width), bf16),
             pltpu.VMEM((rows, width), bf16),
+            pltpu.VMEM((rows, width), bf16),
             pltpu.VMEM((rows, width), f32),
             pltpu.VMEM((rows, width), bf16),
+            pltpu.VMEM((rows, width), f32),
             pltpu.VMEM((rows // BLOCK, BLOCK, BLOCK), f32),
+            pltpu.SemaphoreType.DMA((4, heads)),
             pltpu.SemaphoreType.DMA((3, heads)),
-            pltpu.SemaphoreType.DMA((2, heads)),
         ],
         compiler_params=pltpu.CompilerParams(vmem_limit_bytes=LIMIT),
         cost_estimate=cost(4 * rows * width * BLOCK, 12 * rows * width, rows * width * 8),
         name="inner",
-    )(request_starts, decay_rate, query, key_in, value_in)
+    )(request_starts, decay_rate, norm_gain.reshape(1, width), query, key_in, value_in, gate_in)
 
     back = pl.pallas_call(
         functools.partial(scan_kernel, rows),
@@ -460,7 +466,7 @@
     normed_output = pl.pallas_call(
         functools.partial(norm_kernel, float(width * groups)),
         out_shape=jax.ShapeDtypeStruct((rows, width), bf16),
-        in_specs=[VMEM, VMEM, VMEM, VMEM],
+        in_specs=[VMEM, VMEM, VMEM],
         out_specs=HBM,
         scratch_shapes=[
             pltpu.VMEM((rows, width), bf16),
@@ -469,7 +475,7 @@
         compiler_params=pltpu.CompilerParams(vmem_limit_bytes=ROOM),
         cost_estimate=cost(6 * rows * width, 8 * MIB, rows * width),
         name="norm",
-    )(shared, norm_gain.reshape(1, width), attended, gate_in)
+    )(shared, attended, gated)
     return (normed_output, final_states.reshape(1, heads, E, E))
 
 

time: 80 us -> 79.5 us (level)
  waiting for transfers between devices: 8.11 us -> 7.06 us
    pallas_call x1, Pallas kernels: 11.1 us -> 12.2 us  [local(): pl.pallas_call(functools.partial(inner_kernel, rows, ranks), out_shape=(j...]
    all_to_all x1, waiting for transfers between devices: 8.11 us -> 7.06 us  [swap(): return lax.all_to_all(array, axis, split_axis=0, concat_axis=0, tiled=True)]
  transfers between devices with their start and end apart: 1 -> 1, of which waited for: 1 -> 1; matrix products, arithmetic and copies ran while one was open for 0% -> 0% of each run, Pallas kernels for 14% -> 15%
where the time goes in v3:
time: 79.5 us; the launch traced here: 79.2 us
  blocking collectives  35.7 us (45%)
  Pallas kernels  23.9 us (30%)
  starting transfers between devices  11.9 us (15%)
  waiting for transfers between devices  7.06 us (9%)
    all_to_all x2, blocking collectives, swap(): return lax.all_to_all(array, axis, split_axis=0, concat_axis=0, tiled=True)  35.7 us
    pallas_call x1, Pallas kernels, local(): pl.pallas_call(functools.partial(inner_kernel, rows, ranks), out_shape=(j...  12.2 us
    all_to_all x1, starting transfers between devices, swap(): return lax.all_to_all(array, axis, split_axis=0, concat_axis=0, tiled=True)  11.9 us
    all_to_all x1, waiting for transfers between devices, swap(): return lax.all_to_all(array, axis, split_axis=0, concat_axis=0, tiled=True)  7.06 us
    pallas_call x1, Pallas kernels, local(): pl.pallas_call(functools.partial(states_kernel, rows, ranks), out_shape=(...  5.87 us
    pallas_call x1, Pallas kernels, local(): pl.pallas_call(functools.partial(outer_kernel, rows, ranks), out_shape=(j...  3.23 us
  transfers between devices with their start and end apart: 1, of which 1 were waited for; matrix products, arithmetic and copies ran while one was open for 0% of the time, Pallas kernels for 15%

profile of v3, /device:TPU:1, one launch (start us, length us, event | category | flops | bytes accessed | tf_op | source)
XLA Modules:
  0.0 79.2 jit_solution(13475771412441370775)
XLA Ops:
  0.6 5.9 %states.1 = (bf16[32,3,32,128]{3,2,1,0:T(8,128)(2,1)}, f32[8,128,128]{2,1,0:T(8,128)}) custom-call(s32[32]{0:T(128)} %starts_ref.5, f32[8]{0:T(128)} %rates_ref.5, bf16[1024,1024]{1,0:T(8,128)(2,1)} %k_hbm.3, bf16[1024,1024]{1,0:T(8,128)(2,1)} %v_hbm.3), custom_call_target="tpu_custom_call" | custom-call | flops 805306368 | bytes 5242880 | tf_op jit(solution)/shard_map/states/pallas_call | solution.py:377
  6.5 11.9 %all-to-all-start = ((bf16[32,3,32,128]{3,2,1,0:T(8,128)(2,1)}), bf16[32,3,32,128]{3,2,1,0:T(8,128)(2,1)S(1)}, u32[]{:S(2)}, u32[]{:S(2)}) async-start(bf16[32,3,32,128]{3,2,1,0:T(8,128)(2,1)} %get-tuple-element.10), calls=%async_computation | async-start | bytes 1572864 | tf_op jit(solution)/shard_map/all_to_all | solution.py:357
  18.4 0.0 copy-start.4
  18.4 0.0 copy-start.5
  18.4 0.0 copy-start.6
  18.4 0.0 copy-start.3
  18.4 12.2 %inner.1 = (f32[1024,1024]{1,0:T(8,128)}, bf16[1024,1024]{1,0:T(8,128)(2,1)}, f32[1024,1024]{1,0:T(8,128)}) custom-call(s32[32]{0:T(128)} %starts_ref.5, f32[8]{0:T(128)} %rates_ref.5, f32[1,1024]{1,0:T(1,128)} %bitcast.3, bf16[1024,1024]{1,0:T(8,128)(2,1)} %q_hbm.1, bf16[1024,1024]{1,0:T(8,128)(2,1)} %k_hbm.3, bf16[1024,1024]{1,0:T(8,128)(2,1)} %v_hbm.3, ...), custom_call_target="tpu_custom_call" | custom-call | flops 2147483648 | bytes 12582912 | tf_op jit(solution)/shard_map/inner/pallas_call | solution.py:405
  30.6 7.1 %all-to-all-done.got_ref = bf16[32,3,32,128]{3,2,1,0:T(8,128)(2,1)S(1)} async-done(((bf16[32,3,32,128]{3,2,1,0:T(8,128)(2,1)}), bf16[32,3,32,128]{3,2,1,0:T(8,128)(2,1)S(1)}, u32[]{:S(2)}, u32[]{:S(2)}) %all-to-all-start) | async-done | bytes 786464 | tf_op jit(solution)/shard_map/all_to_all | solution.py:357
  37.6 0.0 copy-done.4
  37.6 0.0 copy-done.5
  37.7 0.0 copy-done.6
  37.7 0.0 copy-start
  37.7 0.0 copy-start.2
  37.7 1.0 %scan.1 = bf16[32,2,32,128]{3,2,1,0:T(8,128)(2,1)S(1)} custom-call(s32[32]{0:T(128)S(1)} %copy-done.4, s32[32]{0:T(128)S(1)} %copy-done.6, f32[8]{0:T(128)S(1)} %copy-done.5, bf16[32,3,32,128]{3,2,1,0:T(8,128)(2,1)S(1)} %all-to-all-done.got_ref, f32[1024,1024]{1,0:T(8,128)} %get-tuple-element.11.inner_hbm.inner_ref), custom_call_target="tpu_custom_call" | custom-call | flops 1048576 | bytes 2097152 | tf_op jit(solution)/shard_map/scan/pallas_call | solution.py:431
  38.7 22.1 %all_to_all.15.back_ref = bf16[32,2,32,128]{3,2,1,0:T(8,128)(2,1)S(1)} all-to-all(bf16[32,2,32,128]{3,2,1,0:T(8,128)(2,1)S(1)} %scan.1), channel_id=1, replica_groups=mesh['ctx'=32,'head'=8] {'ctx'}, dimensions={0} | all-to-all | bytes 1048576 | tf_op jit(solution)/shard_map/all_to_all | solution.py:357
  60.9 0.0 copy-done.3
  60.9 0.0 copy-done
  60.9 0.0 copy-done.2
  60.9 0.0 copy-start.1
  60.9 3.2 %outer.1 = (f32[1024,1024]{1,0:T(8,128)S(1)}, bf16[32,32,128]{2,1,0:T(8,128)(2,1)}, f32[8,8,128]{2,1,0:T(8,128)S(1)}) custom-call(s32[32]{0:T(128)S(1)} %copy-done.4, f32[8]{0:T(128)S(1)} %copy-done.5, bf16[32,2,32,128]{3,2,1,0:T(8,128)(2,1)S(1)} %all_to_all.15.back_ref, f32[8,128,128]{2,1,0:T(8,128)S(1)} %copy-done.3, ...), custom_call_target="tpu_custom_call", output_to_operand_aliasing={{0}: (5, {})} | custom-call | flops 268435456 | bytes 10485760 | tf_op jit(solution)/shard_map/outer/pallas_call | solution.py:444
  64.1 13.5 %all_to_all.16.squares_ref = f32[8,8,128]{2,1,0:T(8,128)S(1)} all-to-all(f32[8,8,128]{2,1,0:T(8,128)S(1)} %get-tuple-element.14), channel_id=1, replica_groups=mesh['ctx'=32,'head'=8] {'head'}, dimensions={0} | all-to-all | bytes 65536 | tf_op jit(solution)/shard_map/all_to_all | solution.py:357
  77.7 0.0 copy-done.1
  77.7 1.6 %norm.1 = bf16[1024,1024]{1,0:T(8,128)(2,1)} custom-call(f32[8,8,128]{2,1,0:T(8,128)S(1)} %all_to_all.16.squares_ref, f32[1024,1024]{1,0:T(8,128)S(1)} %get-tuple-element.15.att_ref, f32[1024,1024]{1,0:T(8,128)S(1)} %copy-done.1), custom_call_target="tpu_custom_call" | custom-call | flops 6291456 | bytes 8388608 | tf_op jit(solution)/shard_map/norm/pallas_call | solution.py:466
Async XLA Ops:
  6.5 31.1 %all-to-all-start = ((bf16[32,3,32,128]{3,2,1,0:T(8,128)(2,1)}), bf16[32,3,32,128]{3,2,1,0:T(8,128)(2,1)S(1)}, u32[]{:S(2)}, u32[]{:S(2)}) async-start(bf16[32,3,32,128]{3,2,1,0:T(8,128)(2,1)} %get-tuple-element.10), calls=%async_computation | async-start | bytes 1572864 | tf_op jit(solution)/shard_map/all_to_all | solution.py:357
  18.4 19.3 %copy-start.4 = (s32[32]{0:T(128)S(1)}, s32[32]{0:T(128)}, u32[]{:S(2)}) copy-start(s32[32]{0:T(128)} %starts_ref.5) | copy-start | bytes 388
  18.4 19.3 %copy-start.5 = (f32[8]{0:T(128)S(1)}, f32[8]{0:T(128)}, u32[]{:S(2)}) copy-start(f32[8]{0:T(128)} %rates_ref.5) | copy-start | bytes 100
  18.4 19.3 %copy-start.6 = (s32[32]{0:T(128)S(1)}, s32[32]{0:T(128)}, u32[]{:S(2)}) copy-start(s32[32]{0:T(128)} %slots_ref.1) | copy-start | bytes 388
  18.4 42.5 %copy-start.3 = (f32[8,128,128]{2,1,0:T(8,128)S(1)}, f32[8,128,128]{2,1,0:T(8,128)}, u32[]{:S(2)}) copy-start(f32[8,128,128]{2,1,0:T(8,128)} %get-tuple-element.12.mid_ref) | copy-start | bytes 1572868
  37.7 23.2 %copy-start = (f32[1024,1024]{1,0:T(8,128)S(1)}, f32[1024,1024]{1,0:T(8,128)}, u32[]{:S(2)}) copy-start(f32[1024,1024]{1,0:T(8,128)} %get-tuple-element.11.inner_hbm.inner_ref) | copy-start | bytes 12582916
  37.7 23.2 %copy-start.2 = (bf16[1024,1024]{1,0:T(8,128)(2,1)S(1)}, bf16[1024,1024]{1,0:T(8,128)(2,1)}, u32[]{:S(2)}) copy-start(bf16[1024,1024]{1,0:T(8,128)(2,1)} %get-tuple-element.13.act_ref) | copy-start | bytes 6291460
  60.9 16.8 %copy-start.1 = (f32[1024,1024]{1,0:T(8,128)S(1)}, f32[1024,1024]{1,0:T(8,128)}, u32[]{:S(2)}) copy-start(f32[1024,1024]{1,0:T(8,128)} %get-tuple-element.16.gated_ref) | copy-start | bytes 12582916

commit v4 on v3

--- a/solution.py
+++ b/solution.py
@@ -75,8 +75,8 @@
 
 
 def states_kernel(
-    rows, ranks, starts_hbm, rates_hbm, k_hbm, v_hbm, sums_hbm, mid_hbm,
-    starts_ref, rates_ref, k_raw, v_raw, gap, upto, sums, mids, sems, arrived, left,
+    rows, ranks, starts_hbm, rates_hbm, k_hbm, v_hbm, sums_hbm,
+    starts_ref, rates_ref, k_raw, v_raw, gap, upto, sums, sems, arrived, left,
 ):
     heads = k_raw.shape[1] // E
     small = (
@@ -95,10 +95,7 @@
 
     def store(head):
         pieces = pl.ds(head * share, share)
-        return (
-            pltpu.make_async_copy(sums.at[pieces], sums_hbm.at[pieces], left.at[0, head]),
-            pltpu.make_async_copy(mids.at[head], mid_hbm.at[head], left.at[1, head]),
-        )
+        return pltpu.make_async_copy(sums.at[pieces], sums_hbm.at[pieces], left.at[head])
 
     for copy in small:
         copy.start()
@@ -113,41 +110,28 @@
     in_b = token <= end_b
     place = lax.broadcasted_iota(jnp.int32, (8, rows), 1)
     place_end = jnp.where(place <= end_a, end_a, jnp.where(place <= end_b, end_b, ABSENT))
-    last = (place // BLOCK) * BLOCK + (BLOCK - 1)
-    gap[...] = (jnp.minimum(place_end, last) - place).astype(f32)
+    gap[...] = (jnp.minimum(place_end, rows - 1) - place).astype(f32)
     upto[0] = jnp.where(in_a, 1.0, 0.0)
     upto[1] = jnp.where(in_b, 1.0, 0.0)
-    at_mid = (end_a < BLOCK - 1).astype(jnp.int32) + (end_b < BLOCK - 1).astype(jnp.int32)
 
     def work(head):
         at = lanes(head)
-        power = power_of(rates_ref, head)
-        parts = []
-        for first in range(0, rows, BLOCK):
-            span = pl.ds(first, BLOCK)
-            keys = silu(k_raw[span, at].T)
-            values = silu_wide(v_raw[span, at])
-            decay = jnp.exp2(gap[:, span] * power)
-            scaled = (keys.astype(f32) * decay[:1, :]).astype(bf16)
-            spread = jnp.concatenate(
-                [
-                    (values * upto[0, span, :]).astype(bf16),
-                    (values * upto[1, span, :]).astype(bf16),
-                    values.astype(bf16),
-                ],
-                axis=1,
-            )
-            running = jnp.dot(scaled, spread, preferred_element_type=f32)
-            until_a, until_b, until_c = (running[:, x * E : (x + 1) * E] for x in range(SEGS))
-            parts.append((until_a, until_b - until_a, until_c - until_b))
-        early, late = parts
-        mid = jnp.zeros((E, E), f32)
-        for x, end in enumerate((end_a, end_b, jnp.int32(ABSENT))):
-            reach = jnp.maximum(jnp.minimum(end, rows - 1) - (BLOCK - 1), 0).astype(f32)
-            total = early[x] * scalar_exp2(reach * power) + late[x]
-            sums[pl.ds(head * share, share), x] = total.astype(bf16).reshape(share, -1, E)
-            mid += early[x] * (at_mid == x).astype(f32)
-        mids[head] = mid
+        decay = jnp.exp2(gap[...] * power_of(rates_ref, head))
+        keys = silu(k_raw[:, at].T)
+        values = silu_wide(v_raw[:, at])
+        scaled = (keys.astype(f32) * decay[:1, :]).astype(bf16)
+        spread = jnp.concatenate(
+            [
+                (values * upto[0]).astype(bf16),
+                (values * upto[1]).astype(bf16),
+                values.astype(bf16),
+            ],
+            axis=1,
+        )
+        running = jnp.dot(scaled, spread, preferred_element_type=f32)
+        until_a, until_b, until_c = (running[:, x * E : (x + 1) * E] for x in range(SEGS))
+        for x, part in enumerate((until_a, until_b - until_a, until_c - until_b)):
+            sums[pl.ds(head * share, share), x] = part.astype(bf16).reshape(share, -1, E)
 
     @pl.loop(0, heads // 2)
     def _(group):
@@ -158,12 +142,10 @@
         for head in mine:
             work(head)
         for head in mine:
-            for copy in store(head):
-                copy.start()
+            store(head).start()
 
     for head in range(heads):
-        for copy in store(head):
-            copy.wait()
+        store(head).wait()
 
 
 def request_ends(starts_ref, rows, ranks):
@@ -249,6 +231,12 @@
         keep = (s <= t) & (s + block * BLOCK >= begin)
         dist[block] = jnp.where(keep, (t - s).astype(f32), FAR)
 
+    place = lax.broadcasted_iota(jnp.int32, (8, BLOCK), 1)
+    begin = jnp.where(
+        BLOCK - 1 <= end_a, 0, jnp.where(BLOCK - 1 <= end_b, end_a + 1, end_b + 1)
+    )
+    gap = jnp.where(place >= begin, (BLOCK - 1 - place).astype(f32), FAR)
+
     @pl.loop(0, heads)
     def _(head):
         at = lanes(head)
@@ -260,6 +248,9 @@
         gated[:, at] = opened * (0.5 * gain_ref[:, at])
         keys = silu(k_raw[:, at])
         values = silu(v_raw[:, at])
+        decay = jnp.exp2(gap * power)
+        turned = (keys[:BLOCK].T.astype(f32) * decay[:1, :]).astype(bf16)
+        inner[pl.ds(rows, E), at] = jnp.dot(turned, values[:BLOCK], preferred_element_type=f32)
         for block in range(rows // BLOCK):
             base = block * BLOCK
             for top in range(0, BLOCK, TILE):
@@ -285,10 +276,10 @@
 
 
 def outer_kernel(
-    rows, ranks, starts_ref, rates_ref, back_ref, mid_ref, act_ref, inner_ref,
-    out_ref, final_hbm, squares_ref, total, lead, left,
-):
-    heads = mid_ref.shape[0]
+    rows, ranks, starts_ref, rates_ref, back_ref, act_ref, inner_ref,
+    out_ref, final_hbm, squares_ref, total, lead, handed, left,
+):
+    heads = inner_ref.shape[1] // E
     share = back_ref.shape[0] // heads
     finals = pltpu.make_async_copy(back_ref.at[:, 1], final_hbm, left.at[0])
     finals.start()
@@ -301,15 +292,18 @@
         here = steps + block * BLOCK <= last
         lead[block] = jnp.where(here, (steps + 1).astype(f32), FAR)
 
+    for head in range(heads):
+        incoming = back_ref[pl.ds(head * share, share), 0].reshape(E, E).astype(f32)
+        whole = scalar_exp2(float(BLOCK) * power_of(rates_ref, head)) * from_before
+        later = inner_ref[pl.ds(rows, E), head * E : (head + 1) * E] + incoming * whole
+        handed[head] = later.astype(bf16)
+
     @pl.loop(0, heads, unroll=4)
     def _(head):
         at = lanes(head)
         power = power_of(rates_ref, head)
         incoming = back_ref[pl.ds(head * share, share), 0].reshape(E, E)
-        later = mid_ref[head] + incoming.astype(f32) * (
-            scalar_exp2(float(BLOCK) * power) * from_before
-        )
-        for block, state in enumerate((incoming, later.astype(bf16))):
+        for block, state in enumerate((incoming, handed[head])):
             span = pl.ds(block * BLOCK, BLOCK)
             outer = jnp.dot(act_ref[span, at], state, preferred_element_type=f32)
             attended = inner_ref[span, at] + outer * jnp.exp2(lead[block] * power)
@@ -374,14 +368,11 @@
     heads = decay_rate.shape[0]
     piece = E * heads // ranks
 
-    sums, mid = pl.pallas_call(
+    sums = pl.pallas_call(
         functools.partial(states_kernel, rows, ranks),
-        out_shape=(
-            jax.ShapeDtypeStruct((ranks, SEGS, piece, E), bf16),
-            jax.ShapeDtypeStruct((heads, E, E), f32),
-        ),
+        out_shape=jax.ShapeDtypeStruct((ranks, SEGS, piece, E), bf16),
         in_specs=[HBM, HBM, HBM, HBM],
-        out_specs=(HBM, HBM),
+        out_specs=HBM,
         scratch_shapes=[
             pltpu.SMEM(request_starts.shape, jnp.int32),
             pltpu.SMEM(decay_rate.shape, f32),
@@ -390,10 +381,9 @@
             pltpu.VMEM((8, rows), f32),
             pltpu.VMEM((ENDS_MOST, rows, E), f32),
             pltpu.VMEM((ranks, SEGS, piece, E), bf16),
-            pltpu.VMEM((heads, E, E), f32),
             pltpu.SemaphoreType.DMA((2,)),
             pltpu.SemaphoreType.DMA((2, heads)),
-            pltpu.SemaphoreType.DMA((2, heads)),
+            pltpu.SemaphoreType.DMA((heads,)),
         ],
         compiler_params=pltpu.CompilerParams(vmem_limit_bytes=LIMIT),
         cost_estimate=cost(2 * rows * width * E * SEGS, 5 * MIB, 3 * rows * width),
@@ -405,7 +395,7 @@
     inner, act, gated = pl.pallas_call(
         functools.partial(inner_kernel, rows, ranks),
         out_shape=(
-            jax.ShapeDtypeStruct((rows, width), f32),
+            jax.ShapeDtypeStruct((rows + E, width), f32),
             jax.ShapeDtypeStruct((rows, width), bf16),
             jax.ShapeDtypeStruct((rows, width), f32),
         ),
@@ -416,7 +406,7 @@
             pltpu.VMEM((rows, width), bf16),
             pltpu.VMEM((rows, width), bf16),
             pltpu.VMEM((rows, width), bf16),
-            pltpu.VMEM((rows, width), f32),
+            pltpu.VMEM((rows + E, width), f32),
             pltpu.VMEM((rows, width), bf16),
             pltpu.VMEM((rows, width), f32),
             pltpu.VMEM((rows // BLOCK, BLOCK, BLOCK), f32),
@@ -444,22 +434,23 @@
     attended, final_states, squares = pl.pallas_call(
         functools.partial(outer_kernel, rows, ranks),
         out_shape=(
-            jax.ShapeDtypeStruct((rows, width), f32),
+            jax.ShapeDtypeStruct((rows + E, width), f32),
             jax.ShapeDtypeStruct((ranks, piece, E), bf16),
             jax.ShapeDtypeStruct((groups, rows // E, E), f32),
         ),
-        in_specs=[SMEM, SMEM, VMEM, VMEM, VMEM, VMEM],
+        in_specs=[SMEM, SMEM, VMEM, VMEM, VMEM],
         out_specs=(VMEM, HBM, VMEM),
         scratch_shapes=[
             pltpu.VMEM((rows, E), f32),
             pltpu.VMEM((rows // BLOCK, BLOCK, E), f32),
+            pltpu.VMEM((heads, E, E), bf16),
             pltpu.SemaphoreType.DMA((1,)),
         ],
-        input_output_aliases={5: 0},
+        input_output_aliases={4: 0},
         compiler_params=pltpu.CompilerParams(vmem_limit_bytes=ROOM),
         cost_estimate=cost(2 * rows * width * E, 10 * MIB, MIB),
         name="outer",
-    )(request_starts, decay_rate, returned, mid, act, inner)
+    )(request_starts, decay_rate, returned, act, inner)
 
     shared = swap(squares, "head")
 

time: 79.5 us -> 79.4 us (level)
  no operation moved by 1% of the time
where the time goes in v4:
time: 79.4 us; the launch traced here: 79.1 us
  blocking collectives  35.7 us (45%)
  Pallas kernels  23.4 us (29%)
  starting transfers between devices  11.9 us (15%)
  waiting for transfers between devices  7.4 us (9%)
    all_to_all x2, blocking collectives, swap(): return lax.all_to_all(array, axis, split_axis=0, concat_axis=0, tiled=True)  35.7 us
    all_to_all x1, starting transfers between devices, swap(): return lax.all_to_all(array, axis, split_axis=0, concat_axis=0, tiled=True)  11.9 us
    pallas_call x1, Pallas kernels, local(): pl.pallas_call(functools.partial(inner_kernel, rows, ranks), out_shape=(j...  11.8 us
    all_to_all x1, waiting for transfers between devices, swap(): return lax.all_to_all(array, axis, split_axis=0, concat_axis=0, tiled=True)  7.4 us
    pallas_call x1, Pallas kernels, local(): pl.pallas_call(functools.partial(states_kernel, rows, ranks), out_shape=j...  5.61 us
    pallas_call x1, Pallas kernels, local(): pl.pallas_call(functools.partial(outer_kernel, rows, ranks), out_shape=(j...  3.41 us
  transfers between devices with their start and end apart: 1, of which 1 were waited for; matrix products, arithmetic and copies ran while one was open for 0% of the time, Pallas kernels for 15%

profile of v4, /device:TPU:1, one launch (start us, length us, event | category | flops | bytes accessed | tf_op | source)
XLA Modules:
  0.0 79.1 jit_solution(11401832773232775543)
XLA Ops:
  0.6 5.6 %states.1 = bf16[32,3,32,128]{3,2,1,0:T(8,128)(2,1)} custom-call(s32[32]{0:T(128)} %starts_ref.5, f32[8]{0:T(128)} %rates_ref.5, bf16[1024,1024]{1,0:T(8,128)(2,1)} %k_hbm.3, bf16[1024,1024]{1,0:T(8,128)(2,1)} %v_hbm.3), custom_call_target="tpu_custom_call" | custom-call | flops 805306368 | bytes 5242880 | tf_op jit(solution)/shard_map/states/pallas_call | solution.py:371
  6.2 11.9 %all-to-all-start = ((bf16[32,3,32,128]{3,2,1,0:T(8,128)(2,1)}), bf16[32,3,32,128]{3,2,1,0:T(8,128)(2,1)S(1)}, u32[]{:S(2)}, u32[]{:S(2)}) async-start(bf16[32,3,32,128]{3,2,1,0:T(8,128)(2,1)} %states.1), calls=%async_computation | async-start | bytes 1572864 | tf_op jit(solution)/shard_map/all_to_all | solution.py:351
  18.1 0.0 copy-start.3
  18.1 0.0 copy-start.4
  18.2 0.0 copy-start.5
  18.2 11.8 %inner.1 = (f32[1152,1024]{1,0:T(8,128)}, bf16[1024,1024]{1,0:T(8,128)(2,1)}, f32[1024,1024]{1,0:T(8,128)}) custom-call(s32[32]{0:T(128)} %starts_ref.5, f32[8]{0:T(128)} %rates_ref.5, f32[1,1024]{1,0:T(1,128)} %bitcast.3, bf16[1024,1024]{1,0:T(8,128)(2,1)} %q_hbm.1, bf16[1024,1024]{1,0:T(8,128)(2,1)} %k_hbm.3, bf16[1024,1024]{1,0:T(8,128)(2,1)} %v_hbm.3, ...), custom_call_target="tpu_custom_call" | custom-call | flops 2147483648 | bytes 12582912 | tf_op jit(solution)/shard_map/inner/pallas_call | solution.py:395
  30.0 7.4 %all-to-all-done.got_ref = bf16[32,3,32,128]{3,2,1,0:T(8,128)(2,1)S(1)} async-done(((bf16[32,3,32,128]{3,2,1,0:T(8,128)(2,1)}), bf16[32,3,32,128]{3,2,1,0:T(8,128)(2,1)S(1)}, u32[]{:S(2)}, u32[]{:S(2)}) %all-to-all-start) | async-done | bytes 786464 | tf_op jit(solution)/shard_map/all_to_all | solution.py:351
  37.4 0.0 copy-done.3
  37.4 0.0 copy-done.4
  37.4 0.0 copy-done.5
  37.4 0.0 copy-start
  37.4 0.0 copy-start.2
  37.4 1.0 %scan.1 = bf16[32,2,32,128]{3,2,1,0:T(8,128)(2,1)S(1)} custom-call(s32[32]{0:T(128)S(1)} %copy-done.3, s32[32]{0:T(128)S(1)} %copy-done.5, f32[8]{0:T(128)S(1)} %copy-done.4, bf16[32,3,32,128]{3,2,1,0:T(8,128)(2,1)S(1)} %all-to-all-done.got_ref, f32[1152,1024]{1,0:T(8,128)} %get-tuple-element.8.inner_hbm.inner_ref), custom_call_target="tpu_custom_call" | custom-call | flops 1048576 | bytes 2097152 | tf_op jit(solution)/shard_map/scan/pallas_call | solution.py:421
  38.4 22.2 %all_to_all.15.back_ref = bf16[32,2,32,128]{3,2,1,0:T(8,128)(2,1)S(1)} all-to-all(bf16[32,2,32,128]{3,2,1,0:T(8,128)(2,1)S(1)} %scan.1), channel_id=1, replica_groups=mesh['ctx'=32,'head'=8] {'ctx'}, dimensions={0} | all-to-all | bytes 1048576 | tf_op jit(solution)/shard_map/all_to_all | solution.py:351
  60.6 0.0 copy-done
  60.6 0.0 copy-done.2
  60.6 0.0 copy-start.1
  60.6 3.4 %outer.1 = (f32[1152,1024]{1,0:T(8,128)S(1)}, bf16[32,32,128]{2,1,0:T(8,128)(2,1)}, f32[8,8,128]{2,1,0:T(8,128)S(1)}) custom-call(s32[32]{0:T(128)S(1)} %copy-done.3, f32[8]{0:T(128)S(1)} %copy-done.4, bf16[32,2,32,128]{3,2,1,0:T(8,128)(2,1)S(1)} %all_to_all.15.back_ref, bf16[1024,1024]{1,0:T(8,128)(2,1)S(1)} %copy-done.2, ...), custom_call_target="tpu_custom_call", output_to_operand_aliasing={{0}: (4, {})} | custom-call | flops 268435456 | bytes 10485760 | tf_op jit(solution)/shard_map/outer/pallas_call | solution.py:434
  64.1 13.5 %all_to_all.16.squares_ref = f32[8,8,128]{2,1,0:T(8,128)S(1)} all-to-all(f32[8,8,128]{2,1,0:T(8,128)S(1)} %get-tuple-element.10), channel_id=1, replica_groups=mesh['ctx'=32,'head'=8] {'head'}, dimensions={0} | all-to-all | bytes 65536 | tf_op jit(solution)/shard_map/all_to_all | solution.py:351
  77.6 0.0 copy-done.1
  77.6 1.6 %norm.1 = bf16[1024,1024]{1,0:T(8,128)(2,1)} custom-call(f32[8,8,128]{2,1,0:T(8,128)S(1)} %all_to_all.16.squares_ref, f32[1152,1024]{1,0:T(8,128)S(1)} %get-tuple-element.11.att_ref, f32[1024,1024]{1,0:T(8,128)S(1)} %copy-done.1), custom_call_target="tpu_custom_call" | custom-call | flops 6291456 | bytes 8388608 | tf_op jit(solution)/shard_map/norm/pallas_call | solution.py:457
Async XLA Ops:
  6.2 31.1 %all-to-all-start = ((bf16[32,3,32,128]{3,2,1,0:T(8,128)(2,1)}), bf16[32,3,32,128]{3,2,1,0:T(8,128)(2,1)S(1)}, u32[]{:S(2)}, u32[]{:S(2)}) async-start(bf16[32,3,32,128]{3,2,1,0:T(8,128)(2,1)} %states.1), calls=%async_computation | async-start | bytes 1572864 | tf_op jit(solution)/shard_map/all_to_all | solution.py:351
  18.1 19.2 %copy-start.3 = (s32[32]{0:T(128)S(1)}, s32[32]{0:T(128)}, u32[]{:S(2)}) copy-start(s32[32]{0:T(128)} %starts_ref.5) | copy-start | bytes 388
  18.1 19.2 %copy-start.4 = (f32[8]{0:T(128)S(1)}, f32[8]{0:T(128)}, u32[]{:S(2)}) copy-start(f32[8]{0:T(128)} %rates_ref.5) | copy-start | bytes 100
  18.2 19.2 %copy-start.5 = (s32[32]{0:T(128)S(1)}, s32[32]{0:T(128)}, u32[]{:S(2)}) copy-start(s32[32]{0:T(128)} %slots_ref.1) | copy-start | bytes 388
  37.4 23.3 %copy-start = (f32[1152,1024]{1,0:T(8,128)S(1)}, f32[1152,1024]{1,0:T(8,128)}, u32[]{:S(2)}) copy-start(f32[1152,1024]{1,0:T(8,128)} %get-tuple-element.8.inner_hbm.inner_ref) | copy-start | bytes 14155780
  37.4 23.2 %copy-start.2 = (bf16[1024,1024]{1,0:T(8,128)(2,1)S(1)}, bf16[1024,1024]{1,0:T(8,128)(2,1)}, u32[]{:S(2)}) copy-start(bf16[1024,1024]{1,0:T(8,128)(2,1)} %get-tuple-element.9.act_ref) | copy-start | bytes 6291460
  60.6 17.0 %copy-start.1 = (f32[1024,1024]{1,0:T(8,128)S(1)}, f32[1024,1024]{1,0:T(8,128)}, u32[]{:S(2)}) copy-start(f32[1024,1024]{1,0:T(8,128)} %get-tuple-element.12.gated_ref) | copy-start | bytes 12582916
